TPU v7x, 256 devices: a whole 4x4x8 slice. The times are simulated.
256 devices in a mesh: grp: 8 (over z_lo, core), lat: 32 (over x, y, z_hi).
Axes of the slice: x: 4, y: 4, z: 8 (z_hi: 2, z_lo: 4; z = z_hi * 4 + z_lo), core: 2. Of those that a mesh axis runs over, the one named last changes fastest.
Arguments:
- spectral_state: bfloat16 [8, 640, 64, 640], P('grp', 'lat'), may hold values from -6 to 6
- cotangent: bfloat16 [8, 640, 64, 640], P('grp', 'lat'), may hold values from -6 to 6
- legendre: bfloat16 [640, 640, 256], P('lat'), as said below
- quadrature: float32 [256], replicated, may hold values from 0.2 to 1
- damping: float32 [32], replicated, may hold values from 0.05 to 20
- physics_in: bfloat16 [512, 32], replicated, may hold values from -1 to 1
- physics_bias: float32 [512], replicated, may hold values from -3 to 3
- physics_out: bfloat16 [32, 512], replicated, may hold values from -0.25 to 0.25
Outputs:
- grad_state: float32 [8, 640, 64, 640], P('grp', 'lat')
- grad_in: float32 [512, 32], replicated
- grad_bias: float32 [512], replicated
- grad_out: float32 [32, 512], replicated
Inputs may be any that keep to these rules, and one draw needn't show every extreme that they name: legendre[m, l, p] is zero for every degree l below the wavenumber m, and generally nonzero otherwise.
All inputs are finite; a program needn't handle non-finite values.
Results may differ from a plain program's by a relative error of at most 0.015.
Values may be sent and summed in bfloat16 or wider, within the bound.
A program may use at most 192 MiB of HBM per device.

v0:
```python
import math

import jax
import jax.numpy as jnp
from jax import lax
from jax.sharding import PartitionSpec as P

NLON = 2560


def implicit_factor(damping, degrees):
    degree = jnp.arange(degrees, dtype=jnp.float32)
    ratio = degree * (degree + 1.0) / (degrees * (degrees + 1.0))
    factor = 1.0 / (1.0 + damping[:, None] * ratio[None, :])
    return jnp.concatenate([factor, factor], axis=0)


def longitude_table(waves, points):
    wave = jnp.arange(waves, dtype=jnp.int32)[:, None]
    place = jnp.arange(points, dtype=jnp.int32)[None, :]
    phase = wave * place % points
    angle = phase.astype(jnp.float32) * (2.0 * math.pi / points)
    scale = math.sqrt(2.0 / points)
    return jnp.stack([jnp.cos(angle) * scale, -jnp.sin(angle) * scale]).astype(jnp.bfloat16)


def to_grid(arrived, table, chans, lat_rows):
    shaped = arrived.reshape(arrived.shape[0], 2, chans, lat_rows)
    return jnp.einsum("mpcf,pml->cfl", shaped, table, preferred_element_type=jnp.float32).astype(
        jnp.bfloat16
    )


def column_physics(physics_in, physics_bias, physics_out, inputs, tendency):
    hidden = jnp.dot(physics_in, inputs, preferred_element_type=jnp.float32) + physics_bias[:, None]
    sigma = jax.nn.sigmoid(hidden)
    activated = (hidden * sigma).astype(jnp.bfloat16)
    upstream = jnp.dot(physics_out.T, tendency, preferred_element_type=jnp.float32)
    slope = sigma * (1.0 + hidden * (1.0 - sigma))
    pre_grad = (upstream * slope).astype(jnp.bfloat16)
    grad_out = jnp.dot(tendency, activated.T, preferred_element_type=jnp.float32)
    grad_in = jnp.dot(pre_grad, inputs.T, preferred_element_type=jnp.float32)
    grad_bias = jnp.sum(pre_grad.astype(jnp.float32), axis=1)
    grid_grad = jnp.dot(physics_in.T, pre_grad, preferred_element_type=jnp.float32).astype(
        jnp.bfloat16
    )
    return (grid_grad, grad_in, grad_bias, grad_out)


def body(
    spectral_state, cotangent, legendre, quadrature, damping, physics_in, physics_bias, physics_out
):
    spectral = spectral_state[0]
    cot_in = cotangent[0]
    width = spectral.shape[1]
    chans = width // 2
    degrees = spectral.shape[2]
    lat_count = lax.axis_size("lat")
    waves = legendre.shape[0] * lat_count
    lat_rows = legendre.shape[2] // lat_count
    points = NLON
    factor = implicit_factor(damping, degrees)
    direct = cot_in.astype(jnp.float32) * factor[None]
    cot_tend = direct.astype(jnp.bfloat16)
    table = longitude_table(waves, points)
    fourier_state = jnp.einsum(
        "mkl,mlf->mkf", spectral, legendre, preferred_element_type=jnp.float32
    ).astype(jnp.bfloat16)
    arrived_state = lax.all_to_all(fourier_state, "lat", split_axis=2, concat_axis=0, tiled=True)
    fourier_cot = (
        jnp.einsum("mkl,mlf->mkf", cot_tend, legendre, preferred_element_type=jnp.float32)
        * quadrature[None, None, :]
    ).astype(jnp.bfloat16)
    arrived_cot = lax.all_to_all(fourier_cot, "lat", split_axis=2, concat_axis=0, tiled=True)
    grid_state = to_grid(arrived_state, table, chans, lat_rows)
    grid_tend = to_grid(arrived_cot, table, chans, lat_rows)
    columns = lat_rows * points
    grid_grad, grad_in, grad_bias, grad_out = column_physics(
        physics_in,
        physics_bias,
        physics_out,
        grid_state.reshape(chans, columns),
        grid_tend.reshape(chans, columns),
    )
    fourier_grad = jnp.einsum(
        "cfl,pml->mpcf",
        grid_grad.reshape(chans, lat_rows, points),
        table,
        preferred_element_type=jnp.float32,
    ).astype(jnp.bfloat16)
    returned = lax.all_to_all(
        fourier_grad.reshape(waves, width, lat_rows), "lat", split_axis=0, concat_axis=2, tiled=True
    )
    grad_state = direct + jnp.einsum(
        "mkf,mlf->mkl", returned, legendre, preferred_element_type=jnp.float32
    )
    totals = lax.psum((grad_in, grad_bias, grad_out), ("grp", "lat"))
    scale = 1.0 / math.sqrt(lax.axis_size("grp") * lat_count * lat_rows * points)
    return (grad_state[None], totals[0] * scale, totals[1] * scale, totals[2] * scale)


def solution(mesh):
    in_specs = (
        P("grp", "lat", None, None),
        P("grp", "lat", None, None),
        P("lat", None, None),
        P(),
        P(),
        P(),
        P(),
        P(),
    )
    out_specs = (P("grp", "lat", None, None), P(), P(), P())
    return jax.shard_map(body, mesh=mesh, in_specs=in_specs, out_specs=out_specs, check_vma=False)
```

profile of v0, /device:TPU:1, one launch (start us, length us, event | category | flops | bytes accessed | tf_op | source)
XLA Modules:
  0.0 486.3 jit_solution(3974654119827165018)
XLA Ops:
  7.2 0.0 copy-start
  7.2 1.4 copy-done
  8.6 5.0 %fusion.48 = bf16[20,64,256]{2,1,0:T(8,128)(2,1)} fusion(bf16[20,640,256]{2,1,0:T(8,128)(2,1)} %param.10, bf16[1,20,64,640]{3,2,1,0:T(8,128)(2,1)S(1)} %copy-done), kind=kOutput, calls=%fused_computation.45 | convolution fusion | flops 419758080 | bytes 8847360 | tf_op jit(solution)/shard_map/mkl,mlf->mkf/dot_general | solution.py:66
  13.6 1.9 copy.42
  15.5 1.7 reshape.114
  17.2 14.5 %all-to-all-start.1 = ((bf16[32,2,5120]{2,1,0:T(2,128)(2,1)}), bf16[32,2,5120]{2,1,0:T(2,128)(2,1)S(1)}, u32[]{:S(2)}, u32[]{:S(2)}) async-start(bf16[32,2,5120]{2,1,0:T(2,128)(2,1)} %reshape.114), calls=%async_computation.1 | async-start | bytes 1310720 | tf_op jit(solution)/shard_map/all_to_all | solution.py:69
  31.7 0.1 add_divide_fusion
  31.9 0.7 copy-done.8
  32.5 4.0 fusion.45
  36.6 1.0 copy.38
  37.6 1.7 reshape.116
  39.3 10.1 %all-to-all-done.1 = bf16[32,2,5120]{2,1,0:T(2,128)(2,1)S(1)} async-done(((bf16[32,2,5120]{2,1,0:T(2,128)(2,1)}), bf16[32,2,5120]{2,1,0:T(2,128)(2,1)S(1)}, u32[]{:S(2)}, u32[]{:S(2)}) %all-to-all-start.1) | async-done | bytes 655392 | tf_op jit(solution)/shard_map/all_to_all | solution.py:69
  49.4 4.8 all-to-all-start
  54.2 28.6 %multiply_convert_fusion = (bf16[1,640,2560]{2,1,0:T(8,128)(2,1)}, bf16[1,640,2560]{2,1,0:T(8,128)(2,1)}) fusion(), kind=kLoop, calls=%fused_computation.24 | loop fusion | flops 22937600 | bytes 6553600 | tf_op jit(solution)/shard_map/convert.2
  82.8 1.3 reshape.115
  84.1 0.2 copy.44
  84.3 3.0 reshape.117
  87.3 1.2 copy.40
  88.6 5.6 %reshape.103 = bf16[640,2,32,8]{2,1,3,0:T(2,128)(2,1)} reshape(bf16[32,20,64,8]{2,3,1,0:T(8,128)(2,1)} %copy.40) | data formatting | bytes 1310720 | tf_op jit(solution)/shard_map/reshape | solution.py:28
  94.2 5.4 %copy.41 = bf16[640,2,32,8]{0,3,1,2:T(8,128)(2,1)} copy(bf16[640,2,32,8]{2,1,3,0:T(2,128)(2,1)} %reshape.103) | data formatting | bytes 1310720 | tf_op jit(solution)/shard_map/reshape | solution.py:28
  99.6 2.1 reshape.105
  101.7 4.7 copy.45
  106.4 0.0 copy-start.4
  106.4 4.9 %fusion.27 = bf16[32,8,2560]{2,1,0:T(8,128)(2,1)S(1)} fusion(bf16[640,2,32,8]{0,3,1,2:T(8,128)(2,1)S(1)} %copy.45, bf16[1,640,2560]{2,1,0:T(8,128)(2,1)} %get-tuple-element.8, bf16[1,640,2560]{2,1,0:T(8,128)(2,1)} %get-tuple-element.9), kind=kOutput, calls=%fused_computation.32 | convolution fusion | flops 1681653760 | bytes 8519680 | tf_op jit(solution)/shard_map/mpcf,pml->cfl/dot_general | solution.py:29
  111.3 0.4 copy.59
  111.8 2.1 fusion.30
  113.9 0.4 copy.58
  114.3 0.0 copy-start.15
  114.3 16.4 %fusion.65 = f32[20480,512]{1,0:T(8,128)} fusion(bf16[32,20480]{1,0:T(8,128)(2,1)S(1)} %bitcast.135, bf16[512,32]{0,1:T(8,128)(2,1)S(1)} %copy-done.11), kind=kOutput, calls=%fused_computation.63 | convolution fusion | flops 671088640 | bytes 43286528 | tf_op jit(solution)/shard_map/dot_general | solution.py:35
  130.7 17.5 %fusion.8 = f32[32,512]{1,0:T(8,128)} fusion(bf16[32,20480]{1,0:T(8,128)(2,1)S(1)} %bitcast.145, f32[20480,512]{1,0:T(8,128)} %fusion.65, f32[512]{0:T(512)S(1)} %copy-done.15), kind=kOutput, calls=%fused_computation.13 | convolution fusion | flops 734003200 | bytes 43321344 | tf_op jit(solution)/shard_map/dot_general | solution.py:41
  148.2 26.4 %convert_reduce_fusion = (f32[512]{0:T(512)S(1)}, bf16[512,20480]{0,1:T(8,128)(2,1)}) fusion(f32[20480,512]{1,0:T(8,128)} %fusion.65, f32[512]{0:T(512)S(1)} %copy-done.15, bf16[32,20480]{1,0:T(8,128)(2,1)S(1)} %bitcast.146, bf16[32,512]{1,0:T(8,128)(2,1)S(1)} %copy-done.14), kind=kOutput, calls=%fused_computation.11 | convolution fusion | flops 796917248 | bytes 64262144 | tf_op jit(solution)/shard_map/dot_general | solution.py:38
  174.6 13.3 %convolution_convert_fusion = bf16[20480,32]{0,1:T(8,128)(2,1)S(1)} fusion(bf16[512,20480]{0,1:T(8,128)(2,1)} %get-tuple-element.7, bf16[512,32]{0,1:T(8,128)(2,1)S(1)} %copy-done.11), kind=kOutput, calls=%fused_computation.12 | convolution fusion | flops 671744000 | bytes 22315008 | tf_op jit(solution)/shard_map/dot_general | solution.py:44
  187.9 0.0 copy-done.5
  188.0 1.9 fusion.57
  189.9 1.0 copy.47
  190.9 2.5 copy.48
  193.4 1.6 reshape.118
  195.0 11.6 %all-to-all-start.2 = ((bf16[32,2,5120]{2,1,0:T(2,128)(2,1)}), bf16[32,2,5120]{2,1,0:T(2,128)(2,1)}, u32[]{:S(2)}, u32[]{:S(2)}) async-start(bf16[32,2,5120]{2,1,0:T(2,128)(2,1)} %reshape.118), calls=%async_computation.2 | async-start | bytes 1310720 | tf_op jit(solution)/shard_map/all_to_all | solution.py:91
  206.5 0.0 all-reduce.3.cloned.1.call-start
  206.6 9.5 %fusion.66 = f32[512,32]{0,1:T(8,128)} fusion(bf16[32,20480]{1,0:T(8,128)(2,1)S(1)} %bitcast.136, bf16[512,20480]{0,1:T(8,128)(2,1)} %get-tuple-element.7), kind=kOutput, calls=%fused_computation.64 | convolution fusion | flops 671088640 | bytes 22347776 | tf_op jit(solution)/shard_map/dot_general | solution.py:42
  216.1 0.0 all-reduce.3.cloned.1.call-update
  216.1 83.9 %psum.22 = f32[512]{0:T(512)S(1)} all-reduce(f32[512]{0:T(512)S(1)} %get-tuple-element.6), channel_id=1, replica_groups=mesh['grp'=8,'lat'=32] {'grp','lat'}, use_global_device_ids=true, to_apply=%region_2.3 | all-reduce | flops 512 | bytes 4096 | tf_op jit(solution)/shard_map/psum | solution.py:97
  300.0 0.6 broadcast_multiply_fusion.2
  300.6 165.4 %all-reduce.3.cloned.1.call-done = (f32[512,32]{0,1:T(8,128)}, f32[32,512]{1,0:T(8,128)}) async-done(((f32[512,32]{0,1:T(8,128)}, f32[32,512]{1,0:T(8,128)}), (f32[512,32]{0,1:T(8,128)}, f32[32,512]{1,0:T(8,128)})) %all-reduce.3.cloned.1.call-update) | async-done | bytes 131088 | tf_op jit(solution)/shard_map/psum | solution.py:97
  466.0 1.5 broadcast_multiply_fusion.1
  467.5 1.5 broadcast_multiply_fusion
  468.9 3.4 reshape.119
  472.3 7.2 %fusion.35 = f32[1,20,64,640]{3,2,1,0:T(8,128)} fusion(bf16[20,640,256]{2,1,0:T(8,128)(2,1)} %param.10, bf16[1,20,64,640]{3,2,1,0:T(8,128)(2,1)S(1)} %copy-done.3, f32[64,640]{1,0:T(8,128)S(1)} %copy-done.9, bf16[20,64,32,8]{1,3,0,2:T(8,128)(2,1)} %bitcast.141), kind=kOutput, calls=%fused_computation.37 | convolution fusion | flops 421888000 | bytes 12288000 | tf_op jit(solution)/shard_map/mkf,mlf->mkl/dot_general | solution.py:94
  (30 shorter events, 0.1 us)
Async XLA Ops:
  7.2 1.4 copy-start
  13.6 18.1 %copy-start.13 = (f32[32]{0:T(128)S(1)}, f32[32]{0:T(128)}, u32[]{:S(2)}) copy-start(f32[32]{0:T(128)} %param.12) | copy-start | bytes 388
  13.6 18.9 %copy-start.2 = (bf16[1,20,64,640]{3,2,1,0:T(8,128)(2,1)S(1)}, bf16[1,20,64,640]{3,2,1,0:T(8,128)(2,1)}, u32[]{:S(2)}) copy-start(bf16[1,20,64,640]{3,2,1,0:T(8,128)(2,1)} %param.9) | copy-start | bytes 4915204
  13.6 18.9 %copy-start.12 = (f32[256]{0:T(256)S(1)}, f32[256]{0:T(256)}, u32[]{:S(2)}) copy-start(f32[256]{0:T(256)} %param.11) | copy-start | bytes 3076
  17.2 32.2 %all-to-all-start.1 = ((bf16[32,2,5120]{2,1,0:T(2,128)(2,1)}), bf16[32,2,5120]{2,1,0:T(2,128)(2,1)S(1)}, u32[]{:S(2)}, u32[]{:S(2)}) async-start(bf16[32,2,5120]{2,1,0:T(2,128)(2,1)} %reshape.114), calls=%async_computation.1 | async-start | bytes 1310720 | tf_op jit(solution)/shard_map/all_to_all | solution.py:69
  31.8 0.7 copy-start.8
  49.4 34.9 %all-to-all-start = ((bf16[32,2,5120]{2,1,0:T(2,128)(2,1)}), bf16[32,2,5120]{2,1,0:T(2,128)(2,1)}, u32[]{:S(2)}, u32[]{:S(2)}) async-start(bf16[32,2,5120]{2,1,0:T(2,128)(2,1)} %reshape.116), calls=%async_computation | async-start | bytes 1310720 | tf_op jit(solution)/shard_map/all_to_all | solution.py:74
  106.4 5.4 %copy-start.4 = (bf16[1,640,2560]{2,1,0:T(8,128)(2,1)S(1)}, bf16[1,640,2560]{2,1,0:T(8,128)(2,1)}, u32[]{:S(2)}) copy-start(bf16[1,640,2560]{2,1,0:T(8,128)(2,1)} %get-tuple-element.8) | copy-start | bytes 9830404
  106.4 5.4 %copy-start.6 = (bf16[1,640,2560]{2,1,0:T(8,128)(2,1)S(1)}, bf16[1,640,2560]{2,1,0:T(8,128)(2,1)}, u32[]{:S(2)}) copy-start(bf16[1,640,2560]{2,1,0:T(8,128)(2,1)} %get-tuple-element.9) | copy-start | bytes 9830404
  106.4 5.4 %copy-start.10 = (bf16[640,2,32,8]{0,3,1,2:T(8,128)(2,1)S(1)}, bf16[640,2,32,8]{0,3,1,2:T(8,128)(2,1)}, u32[]{:S(2)}) copy-start(bf16[640,2,32,8]{0,3,1,2:T(8,128)(2,1)} %copy.41) | copy-start | bytes 1966084
  111.8 2.5 copy-start.11
  114.3 16.4 %copy-start.15 = (f32[512]{0:T(512)S(1)}, f32[512]{0:T(512)}, u32[]{:S(2)}) copy-start(f32[512]{0:T(512)} %param.14) | copy-start | bytes 6148
  130.7 17.5 %copy-start.14 = (bf16[32,512]{1,0:T(8,128)(2,1)S(1)}, bf16[32,512]{1,0:T(8,128)(2,1)}, u32[]{:S(2)}) copy-start(bf16[32,512]{1,0:T(8,128)(2,1)} %param.15) | copy-start | bytes 98308
  174.6 13.3 %copy-start.5 = (bf16[1,640,2560]{2,1,0:T(8,128)(2,1)S(1)}, bf16[1,640,2560]{2,1,0:T(8,128)(2,1)}, u32[]{:S(2)}) copy-start(bf16[1,640,2560]{2,1,0:T(8,128)(2,1)} %get-tuple-element.8) | copy-start | bytes 9830404
  174.6 13.3 %copy-start.7 = (bf16[1,640,2560]{2,1,0:T(8,128)(2,1)S(1)}, bf16[1,640,2560]{2,1,0:T(8,128)(2,1)}, u32[]{:S(2)}) copy-start(bf16[1,640,2560]{2,1,0:T(8,128)(2,1)} %get-tuple-element.9) | copy-start | bytes 9830404
  195.0 274.0 %all-to-all-start.2 = ((bf16[32,2,5120]{2,1,0:T(2,128)(2,1)}), bf16[32,2,5120]{2,1,0:T(2,128)(2,1)}, u32[]{:S(2)}, u32[]{:S(2)}) async-start(bf16[32,2,5120]{2,1,0:T(2,128)(2,1)} %reshape.118), calls=%async_computation.2 | async-start | bytes 1310720 | tf_op jit(solution)/shard_map/all_to_all | solution.py:91
  206.5 265.8 %copy-start.9 = (f32[64,640]{1,0:T(8,128)S(1)}, f32[64,640]{1,0:T(8,128)}, u32[]{:S(2)}) copy-start(f32[64,640]{1,0:T(8,128)} %copy-done.8) | copy-start | bytes 491524
  206.5 259.4 %all-reduce.3.cloned.1.call-start = ((), (), s32[]{:S(2)}) async-start(), calls=%async_computation.3 | async-start | bytes 262144 | tf_op jit(solution)/shard_map/psum | solution.py:97
  216.1 256.2 %copy-start.3 = (bf16[1,20,64,640]{3,2,1,0:T(8,128)(2,1)S(1)}, bf16[1,20,64,640]{3,2,1,0:T(8,128)(2,1)}, u32[]{:S(2)}) copy-start(bf16[1,20,64,640]{3,2,1,0:T(8,128)(2,1)} %param.9) | copy-start | bytes 4915204
  472.3 7.2 %copy-start.1 = (bf16[1,20,64,640]{3,2,1,0:T(8,128)(2,1)S(1)}, bf16[1,20,64,640]{3,2,1,0:T(8,128)(2,1)}, u32[]{:S(2)}) copy-start(bf16[1,20,64,640]{3,2,1,0:T(8,128)(2,1)} %param.8) | copy-start | bytes 4915204
Sparse Core Ops, SparseCore 0:
  216.3 249.6 all-reduce.2
where the time goes:
time: 488 us; the launch traced here: 486 us
  waiting for transfers between devices  175 us (36%)
  matrix products  108 us (22%)
  blocking collectives  83.9 us (17%)
  local copies, waits for them, and re-layouts  41.3 us (8%)
  other arithmetic  32.2 us (7%)
  starting transfers between devices  30.9 us (6%)
  between operations  14.3 us (3%)
    psum x1, waiting for transfers between devices, body(): totals = lax.psum((grad_in, grad_bias, grad_out), ('grp', 'lat'))  165 us
    psum x1, blocking collectives, body(): totals = lax.psum((grad_in, grad_bias, grad_out), ('grp', 'lat'))  83.9 us
    another operation x1, other arithmetic  28.6 us
    dot_general x1, matrix products, column_physics(): jnp.dot(physics_out.T, tendency, preferred_element_type=jnp.float32)  26.4 us
    reshape x4, local copies, waits for them, and re-layouts, to_grid(): shaped = arrived.reshape(arrived.shape[0], 2, chans, lat_rows)  17.8 us
    dot_general x1, matrix products, column_physics(): jnp.dot(tendency, activated.T, preferred_element_type=jnp.float32)  17.5 us
    dot_general x1, matrix products, column_physics(): jnp.dot(physics_in, inputs, preferred_element_type=jnp.float32)  16.4 us
    unnamed x40, local copies, waits for them, and re-layouts  15.6 us
  transfers between devices with their start and end apart: 4, of which 2 were waited for; matrix products, arithmetic and copies ran while one was open for 10% of the time, Pallas kernels for 0%

commit v1 on v0

v1 whole, which is shorter than its diff:
```python
import functools
import math

import jax
import jax.numpy as jnp
import ml_dtypes
import numpy as np
from jax import lax
from jax.experimental import pallas as pl
from jax.experimental.pallas import tpu as pltpu
from jax.sharding import PartitionSpec as P

NLON = 2560
HALF = NLON // 2
MESH = pl.DeviceIdType.MESH
F32, BF16 = jnp.float32, jnp.bfloat16

LAT = 32
GRP = 8
XY = 16
MB = 20
HB = MB // 2
NL = 640
NP = 256
CH = 32
HID = 512
COLS = 640
JT = 640
SEND = ((0, 48), (48, 80), (80, 128), (128, 160))
BACK = ((0, 32), (32, 48), (48, 80))
GR = 17


def table_rows(e):
    if e < 8:
        base = 256 * (e // 4) + LAT * (e % 4)
        return base, base + 128
    return 512 + LAT * (e - 8), 576 + LAT * (e - 8)


def longitude_tables():
    place = np.arange(HALF, dtype=np.int64)[:, None]
    owner = np.arange(LAT, dtype=np.int64)[None, :]
    tables = np.zeros((2, HALF, COLS), np.float64)
    scale = math.sqrt(2.0 / NLON)
    for parity in range(2):
        for e in range(HB):
            wave = MB * owner + 2 * e + parity
            angle = (wave * place % NLON) * (2.0 * math.pi / NLON)
            c, s = table_rows(e)
            tables[parity, :, c : c + LAT] = np.cos(angle) * scale
            tables[parity, :, s : s + LAT] = -np.sin(angle) * scale
    return tables.astype(ml_dtypes.bfloat16)


def dot(a, b, ca, cb):
    return lax.dot_general(a, b, (((ca,), (cb,)), ((), ())), preferred_element_type=F32)


def kernel(
    spec_hbm, cot_hbm, leg_hbm, tab_hbm, quad_ref, damp_ref, pin_ref, bias_ref, pout_ref,
    out_hbm, og_ref, ob_ref,
    spec, cot, leg, tab, factor, ft, stage, snd, rcv, rf, wdft, wp, w1t, racc, rall, bsnd, brcv,
    gp, ga, gsnd, g1, g2s, g2r, g3s, g3r, g4s, g4r, outb,
    in_sem, tab_sem, f_s, f_r, b_s, b_r, g_s, g_r, out_sem,
):
    me = lax.axis_index("lat")
    grp = lax.axis_index("grp")
    xy = me // 2

    def peer(k):
        return lax.rem(me + k, LAT)

    barrier = pltpu.get_barrier_semaphore()

    @pl.loop(1, LAT)
    def _(k):
        pl.semaphore_signal(barrier, inc=1, device_id={"lat": peer(k)}, device_id_type=MESH)

    @pl.loop(1, GRP)
    def _(k):
        pl.semaphore_signal(
            barrier, inc=1, device_id={"grp": lax.rem(grp + k, GRP)}, device_id_type=MESH
        )

    def wave(mm):
        return 2 * lax.rem(mm, HB) + mm // HB

    def loads(mm):
        m = wave(mm)
        return [
            pltpu.make_async_copy(src.at[m], dst.at[m], in_sem.at[i, mm])
            for i, (src, dst) in enumerate(((spec_hbm, spec), (cot_hbm, cot), (leg_hbm, leg)))
        ]

    @pl.loop(0, MB)
    def _(mm):
        for copy in loads(mm):
            copy.start()

    tab_copy = pltpu.make_async_copy(tab_hbm, tab, tab_sem)
    tab_copy.start()

    degree = lax.broadcasted_iota(jnp.int32, (CH, NL), 1).astype(F32)
    ratio = degree * (degree + 1.0) / (NL * (NL + 1.0))
    factor[...] = 1.0 / (1.0 + damp_ref[...] * ratio)

    @pl.loop(0, MB)
    def _(mm):
        m = wave(mm)
        for copy in loads(mm):
            copy.wait()
        fac = factor[...]
        s = spec[m]
        c = cot[m].astype(F32)
        c_re = (c[:CH] * fac).astype(BF16)
        c_im = (c[CH:] * fac).astype(BF16)
        lhs = jnp.concatenate([s[:CH], c_re, s[CH:], c_im], axis=0)
        four = dot(lhs, leg[m], 1, 0)
        quad = quad_ref[...]
        four = jnp.concatenate(
            [four[:32], four[32:64] * quad, four[64:96], four[96:] * quad], axis=0
        )
        ft[pl.ds(pl.multiple_of(mm * NP, NP), NP), :] = four.T

    pl.semaphore_wait(barrier, LAT - 1 + GRP - 1)

    def assemble(pair, d):
        for j in range(4):
            row = 128 * (j % 2) + 32 * (2 * pair + j // 2) + d
            stage[pl.ds(MB * j, MB), :] = ft[pl.ds(row, MB, stride=NP), :]
        snd[d, pl.ds(80 * pair, 80), :] = stage[...].astype(BF16)

    def send(c, d):
        lo, hi = SEND[c]
        pltpu.make_async_remote_copy(
            src_ref=snd.at[d, pl.ds(lo, hi - lo)],
            dst_ref=rcv.at[me, pl.ds(lo, hi - lo)],
            send_sem=f_s.at[c],
            recv_sem=f_r.at[c],
            device_id={"lat": d},
            device_id_type=MESH,
        ).start()

    def keep(c):
        lo, hi = SEND[c]
        pltpu.make_async_copy(
            snd.at[me, pl.ds(lo, hi - lo)], rcv.at[me, pl.ds(lo, hi - lo)], f_r.at[c]
        ).start()

    def far_then_near(f):
        @pl.loop(0, LAT // 2)
        def _(i):
            f(peer(2 * i + 1))

        @pl.loop(1, LAT // 2)
        def _(i):
            f(peer(2 * i))

    def pack_send(pair, c):
        def f(d):
            assemble(pair, d)
            send(c, d)

        return f

    far_then_near(pack_send(0, 0))
    assemble(0, me)
    keep(0)
    far_then_near(functools.partial(send, 1))
    keep(1)

    @pl.loop(0, LAT)
    def _(d):
        assemble(1, d)

    wp[...] = jnp.zeros_like(wp)
    w_in = pin_ref[...].astype(F32).T
    w1t[...] = w_in.astype(BF16)
    half_in = (0.5 * w_in).astype(BF16)
    half_out = (0.5 * pout_ref[...].astype(F32)).astype(BF16)
    half_bias = 0.5 * bias_ref[...]
    top = half_bias.astype(BF16).astype(F32)
    mid = (half_bias - top).astype(BF16).astype(F32)
    low = half_bias - top - mid
    row = lax.broadcasted_iota(jnp.int32, (16, HID), 0)
    bias_rows = jnp.where(
        row == 0, top, jnp.where(row == 1, mid, jnp.where(row == 2, low, 0.0))
    ).astype(BF16)
    for s in range(2):
        wp[s, pl.ds(64 * s, CH), pl.ds(0, HID)] = half_in
        wp[s, pl.ds(64 * s + CH, CH), pl.ds(HID, HID)] = half_out
        wp[s, pl.ds(128, 16), pl.ds(0, HID)] = bias_rows
    gp[...] = jnp.zeros_like(gp)
    ga[...] = jnp.zeros_like(ga)
    tab_copy.wait()

    lane = lax.broadcasted_iota(jnp.int32, (LAT, 128), 1)
    left = lane < 64

    def arrive(c):
        lo, hi = SEND[c]
        span = rcv.at[:, pl.ds(lo, hi - lo)]
        pltpu.make_async_copy(span, span, f_r.at[c]).wait()

        at = lo % 80

        @pl.loop(0, LAT)
        def _(src):
            rf[pl.ds(pl.multiple_of(src * 80 + at, 8), hi - lo), :] = rcv[
                src, pl.ds(lo, hi - lo), :
            ].astype(F32)

        first = 40 * (c % 2)
        for mm in range(MB):
            w0 = rf[pl.ds(first + mm, LAT, stride=80), :]
            w1 = rf[pl.ds(first + MB + mm, LAT, stride=80), :]
            re = jnp.where(left, w0, pltpu.roll(w1, 64, 1))
            im = jnp.where(left, pltpu.roll(w0, 64, 1), w1)
            r_re, r_im = table_rows(mm % HB)
            wdft[mm // HB, pl.ds(r_re, LAT), :] = re.astype(BF16)
            wdft[mm // HB, pl.ds(r_im, LAT), :] = im.astype(BF16)

    one_lane = lax.broadcasted_iota(jnp.int32, (2 * JT, 128), 1)
    ones = jnp.where(one_lane < 3, 1.0, 0.0).astype(BF16)
    ones_t = jnp.ones((16, 2 * JT), BF16)

    def physics(i, _):
        span = pl.ds(pl.multiple_of(i * JT, JT), JT)
        even = dot(tab[0, span, :], wdft[0], 1, 0)
        odd = dot(tab[1, span, :], wdft[1], 1, 0)
        x = jnp.concatenate([(even + odd).astype(BF16), (even - odd).astype(BF16)], axis=0)
        xe = jnp.concatenate([x, ones], axis=1)
        xt = x.T
        grads = []
        for s in range(2):
            h = dot(xe, wp[s, :, pl.ds(0, HID)], 1, 0)
            u = dot(xe, wp[s, :, pl.ds(HID, HID)], 1, 0)
            a = 1.0 + jnp.tanh(h)
            act = h * a
            pre = (u * (a * ((1.0 + (h + h)) - act))).astype(BF16)
            act = act.astype(BF16)
            grads.append(dot(w1t[...], pre, 1, 1))
            lhs = jnp.concatenate([xt[64 * s : 64 * s + CH], ones_t], axis=0)
            gp[...] += dot(lhs, pre, 1, 0)
            ga[...] += dot(xt[64 * s + CH : 64 * s + 64], act, 1, 0)
        gg = jnp.concatenate(grads, axis=0)
        g_even = (gg[:, :JT] + gg[:, JT:]).astype(BF16)
        g_odd = (gg[:, :JT] - gg[:, JT:]).astype(BF16)
        racc[0] += dot(g_even, tab[0, span, :], 1, 0)
        racc[1] += dot(g_odd, tab[1, span, :], 1, 0)
        return 0

    def turn(c):
        for parity in range(2):
            r = racc[parity]
            base = 640 * c + 320 * parity
            rall[pl.ds(base, 128), :] = jnp.concatenate([r[:, :128], r[:, 128:256]], axis=0).T
            rall[pl.ds(base + 128, 128), :] = jnp.concatenate(
                [r[:, 256:384], r[:, 384:512]], axis=0
            ).T
            last = r[:, 512:]
            both = jnp.concatenate([last, pltpu.roll(last, 64, 1)], axis=0).T
            rall[pl.ds(base + 256, 64), :] = both[:64]

    def back(n):
        lo, hi = BACK[n]
        first = lo // MB
        last = (hi - 1) // MB

        def pack(d):
            for q in range(first, last + 1):
                stage[pl.ds(MB * q, MB), :] = rall[pl.ds(640 * q + d, MB, stride=LAT), :]
            bsnd[d, pl.ds(lo, hi - lo), :] = stage[pl.ds(lo, hi - lo), :].astype(BF16)

        def go(d):
            pack(d)
            pltpu.make_async_remote_copy(
                src_ref=bsnd.at[d, pl.ds(lo, hi - lo)],
                dst_ref=brcv.at[me, pl.ds(lo, hi - lo)],
                send_sem=b_s.at[n],
                recv_sem=b_r.at[n],
                device_id={"lat": d},
                device_id_type=MESH,
            ).start()

        far_then_near(go)
        pack(me)
        pltpu.make_async_copy(
            bsnd.at[me, pl.ds(lo, hi - lo)], brcv.at[me, pl.ds(lo, hi - lo)], b_r.at[n]
        ).start()

    def xy_step(n, src, dst, mine):
        @pl.loop(1, XY)
        def _(i):
            d = peer(2 * i)
            pltpu.make_async_remote_copy(
                src_ref=src(d // 2),
                dst_ref=dst.at[xy],
                send_sem=g_s.at[n],
                recv_sem=g_r.at[n],
                device_id={"lat": d},
                device_id_type=MESH,
            ).start()

        pltpu.make_async_copy(src(mine), dst.at[xy], g_r.at[n]).start()

    def reduce_1():
        for e in range(XY):
            block, tile = e // 4, e % 4
            cols = pl.ds(128 * tile, 128)
            if block < 2:
                gsnd[e, pl.ds(0, 16), :] = gp[pl.ds(16 * block, 16), cols]
            else:
                gsnd[e, pl.ds(0, 16), :] = ga[pl.ds(16 * (block - 2), 16), cols]
            gsnd[e, pl.ds(16, 1), :] = gp[pl.ds(CH, 1), cols]
        xy_step(0, lambda e: gsnd.at[e], g1, xy)

    def reduce_2():
        pltpu.make_async_copy(g1, g1, g_r.at[0]).wait()
        total = g1[0]
        for e in range(1, XY):
            total = total + g1[e]
        g2s[...] = total
        copy = pltpu.make_async_remote_copy(
            src_ref=g2s,
            dst_ref=g2r,
            send_sem=g_s.at[1],
            recv_sem=g_r.at[1],
            device_id={"lat": me + 1 - 2 * lax.rem(me, 2)},
            device_id_type=MESH,
        )
        copy.start()

    def reduce_3():
        pltpu.make_async_copy(g2r, g2r, g_r.at[1]).wait()
        g3s[...] = g2s[...] + g2r[...]

        @pl.loop(1, GRP)
        def _(k):
            pltpu.make_async_remote_copy(
                src_ref=g3s,
                dst_ref=g3r.at[grp],
                send_sem=g_s.at[2],
                recv_sem=g_r.at[2],
                device_id={"grp": lax.rem(grp + k, GRP)},
                device_id_type=MESH,
            ).start()

        pltpu.make_async_copy(g3s, g3r.at[grp], g_r.at[2]).start()

    def reduce_4():
        pltpu.make_async_copy(g3r, g3r, g_r.at[2]).wait()
        total = g3r[0]
        for e in range(1, GRP):
            total = total + g3r[e]
        g4s[...] = total
        xy_step(3, lambda e: g4s, g4r, xy)

    def reduce_5():
        pltpu.make_async_copy(g4r, g4r, g_r.at[3]).wait()
        for e in range(XY):
            block, tile = e // 4, e % 4
            cols = pl.ds(128 * tile, 128)
            og_ref[pl.ds(16 * block, 16), cols] = g4r[e, pl.ds(0, 16), :]
            if block == 0:
                ob_ref[:, cols] = g4r[e, pl.ds(16, 1), :]

    @pl.loop(0, 4)
    def _(c):
        for now in range(4):

            @pl.when(c == now)
            def _():
                arrive(now)
                if now < 2:
                    far_then_near(functools.partial(send, now + 2))
                    keep(now + 2)

        racc[...] = jnp.zeros_like(racc)
        lax.fori_loop(0, HALF // JT, physics, 0)
        for now in range(4):

            @pl.when(c == now)
            def _():
                if now == 3:
                    reduce_1()
                turn(now)
                if now > 0:
                    back(now - 1)

    def unpack(n):
        lo, hi = BACK[n]
        span = brcv.at[:, pl.ds(lo, hi - lo)]
        pltpu.make_async_copy(span, span, b_r.at[n]).wait()

        @pl.loop(0, LAT)
        def _(src):
            rf[pl.ds(pl.multiple_of(src * 80 + lo, 8), hi - lo), :] = brcv[
                src, pl.ds(lo, hi - lo), :
            ].astype(F32)

    def inverse(mm, _):
        m = wave(mm)
        rows = jnp.concatenate(
            [rf[pl.ds(MB * q + mm, LAT, stride=80), :] for q in range(4)], axis=0
        )
        t = rows.T.astype(BF16)
        lhs = jnp.concatenate(
            [
                jnp.concatenate([t[:32], t[64:96]], axis=0),
                jnp.concatenate([t[32:64], t[96:]], axis=0),
            ],
            axis=1,
        )
        fac = factor[...]
        direct = cot[m].astype(F32) * jnp.concatenate([fac, fac], axis=0)
        outb[m] = direct + dot(lhs, leg[m], 1, 1)
        pltpu.make_async_copy(outb.at[m], out_hbm.at[m], out_sem).start()
        return 0

    unpack(0)
    unpack(1)
    reduce_2()
    reduce_3()
    unpack(2)
    reduce_4()
    lax.fori_loop(0, MB, inverse, 0)
    reduce_5()

    pltpu.make_async_copy(outb, out_hbm, out_sem).wait()
    for c, (lo, hi) in enumerate(SEND):
        span = snd.at[pl.ds(0, LAT - 1), pl.ds(lo, hi - lo)]
        pltpu.make_async_copy(span, span, f_s.at[c]).wait()
    for n, (lo, hi) in enumerate(BACK):
        span = bsnd.at[pl.ds(0, LAT - 1), pl.ds(lo, hi - lo)]
        pltpu.make_async_copy(span, span, b_s.at[n]).wait()
    for n, count, buf in ((0, XY - 1, g1), (2, GRP - 1, g3r), (3, XY - 1, g4r)):
        span = buf.at[pl.ds(0, count)]
        pltpu.make_async_copy(span, span, g_s.at[n]).wait()
    pltpu.make_async_copy(g2s, g2s, g_s.at[1]).wait()


def body(
    tables,
    spectral_state, cotangent, legendre, quadrature, damping, physics_in, physics_bias, physics_out,
):
    hbm = pl.BlockSpec(memory_space=pl.ANY)
    vmem = pl.BlockSpec(memory_space=pltpu.VMEM)
    dma = pltpu.SemaphoreType.DMA
    scratch = [
        pltpu.VMEM((MB, 2 * CH, NL), BF16),
        pltpu.VMEM((MB, 2 * CH, NL), BF16),
        pltpu.VMEM((MB, NL, NP), BF16),
        pltpu.VMEM((2, HALF, COLS), BF16),
        pltpu.VMEM((CH, NL), F32),
        pltpu.VMEM((MB * NP, 128), F32),
        pltpu.VMEM((80, 128), F32),
        pltpu.VMEM((LAT, 160, 128), BF16),
        pltpu.VMEM((LAT, 160, 128), BF16),
        pltpu.VMEM((LAT * 80, 128), F32),
        pltpu.VMEM((2, COLS, 128), BF16),
        pltpu.VMEM((2, 256, 2 * HID), BF16),
        pltpu.VMEM((CH, HID), BF16),
        pltpu.VMEM((2, 64, COLS), F32),
        pltpu.VMEM((4 * 640, 128), F32),
        pltpu.VMEM((LAT, 80, 128), BF16),
        pltpu.VMEM((LAT, 80, 128), BF16),
        pltpu.VMEM((48, HID), F32),
        pltpu.VMEM((CH, HID), F32),
        pltpu.VMEM((XY, GR, 128), F32),
        pltpu.VMEM((XY, GR, 128), F32),
        pltpu.VMEM((GR, 128), F32),
        pltpu.VMEM((GR, 128), F32),
        pltpu.VMEM((GR, 128), F32),
        pltpu.VMEM((GRP, GR, 128), F32),
        pltpu.VMEM((GR, 128), F32),
        pltpu.VMEM((XY, GR, 128), F32),
        pltpu.VMEM((MB, 2 * CH, NL), F32),
        dma((3, MB)),
        dma,
        dma((4,)),
        dma((4,)),
        dma((3,)),
        dma((3,)),
        dma((4,)),
        dma((4,)),
        dma,
    ]
    grad_state, grads, grad_bias = pl.pallas_call(
        kernel,
        out_shape=[
            jax.ShapeDtypeStruct((MB, 2 * CH, NL), F32),
            jax.ShapeDtypeStruct((2 * CH, HID), F32),
            jax.ShapeDtypeStruct((1, HID), F32),
        ],
        in_specs=[hbm] * 4 + [vmem] * 5,
        out_specs=[hbm, vmem, vmem],
        scratch_shapes=scratch,
        compiler_params=pltpu.CompilerParams(
            collective_id=0, has_side_effects=True, vmem_limit_bytes=60 * 2**20
        ),
    )(
        spectral_state[0],
        cotangent[0],
        legendre,
        tables,
        quadrature[None, :],
        damping[:, None],
        physics_in,
        physics_bias[None, :],
        physics_out,
    )
    scale = 1.0 / math.sqrt(GRP * NP * NLON)
    return (grad_state[None], grads[:CH].T * scale, grad_bias[0] * scale, grads[CH:] * scale)


def solution(mesh):
    in_specs = (
        P(),
        P("grp", "lat", None, None),
        P("grp", "lat", None, None),
        P("lat", None, None),
        P(),
        P(),
        P(),
        P(),
        P(),
    )
    out_specs = (P("grp", "lat", None, None), P(), P(), P())
    mapped = jax.shard_map(body, mesh=mesh, in_specs=in_specs, out_specs=out_specs, check_vma=False)
    tables = longitude_tables()

    def run(*args):
        return mapped(jnp.asarray(tables), *args)

    return run
```

time: 488 us -> 104 us (0.21)
  waiting for transfers between devices: 175 us -> 0 us
  matrix products: 108 us -> 0 us
  Pallas kernels: 0 us -> 93.3 us
  blocking collectives: 83.9 us -> 0 us
  local copies, waits for them, and re-layouts: 41.3 us -> 6.82 us
  starting transfers between devices: 30.9 us -> 0 us
  other arithmetic: 32.2 us -> 2.79 us
  between operations: 14.3 us -> 0.64 us
    psum x1 -> x0, waiting for transfers between devices: 165 us -> none  [body(): totals = lax.psum((grad_in, grad_bias, grad_out), ('grp', 'lat'))]
    dot_general x11 -> x0, matrix products: 108 us -> none  [the longest x1 26.4 us: column_physics(): jnp.dot(physics_out.T, tendency, preferred_element_type=jnp.float32)]
    pallas_call x0 -> x1, Pallas kernels: none -> 93.3 us  [body(): pl.pallas_call(kernel, out_shape=[jax.ShapeDtypeStruct((MB, 2 * CH, NL),...]
    psum x1 -> x0, blocking collectives: 83.9 us -> none  [body(): totals = lax.psum((grad_in, grad_bias, grad_out), ('grp', 'lat'))]
    all_to_all x3 -> x0, starting transfers between devices: 30.9 us -> none  [the longest x1 14.5 us: body(): lax.all_to_all(fourier_state, 'lat', split_axis=2, concat_axis=0, tiled=T...]
    another operation x1 -> x0, other arithmetic: 28.6 us -> none
    reshape x5 -> x0, local copies, waits for them, and re-layouts: 20.3 us -> none  [the longest x4 17.8 us: to_grid(): shaped = arrived.reshape(arrived.shape[0], 2, chans, lat_rows)]
    all_to_all x3 -> x0, waiting for transfers between devices: 10.1 us -> none  [the longest x1 10.1 us: body(): lax.all_to_all(fourier_state, 'lat', split_axis=2, concat_axis=0, tiled=T...]
  transfers between devices with their start and end apart: 4 -> 0, of which waited for: 2 -> 0; matrix products, arithmetic and copies ran while one was open for 10% -> 0% of each run, Pallas kernels for 0% -> 0%
where the time goes in v1:
time: 104 us
  Pallas kernels  93.3 us (90%)
  local copies, waits for them, and re-layouts  6.82 us (7%)
  other arithmetic  2.79 us (3%)
    pallas_call x1, Pallas kernels, body(): pl.pallas_call(kernel, out_shape=[jax.ShapeDtypeStruct((MB, 2 * CH, NL),...  93.3 us
    unnamed x2, local copies, waits for them, and re-layouts  5.48 us

profile of v1, /device:TPU:1, one launch (start us, length us, event | category | flops | bytes accessed | tf_op | source)
XLA Modules:
  0.0 103.6 jit_solution(13461357144843866757)
XLA Ops:
  0.6 1.3 %copy.13.damp_ref = f32[32,1]{1,0:T(8,128)} copy(f32[32,1]{0,1:T(1,128)} %bitcast.15) | data formatting | bytes 256 | tf_op jit(solution)/shard_map/broadcast_in_dim | solution.py:509
  2.0 1.5 %copy.14.pin_ref = bf16[512,32]{1,0:T(8,128)(2,1)} copy(bf16[512,32]{0,1:T(8,128)(2,1)} %param.14) | data formatting | bytes 65536 | tf_op args[5]
  3.5 93.3 %shard_map.120 = (f32[20,64,640]{2,1,0:T(8,128)}, f32[64,512]{1,0:T(8,128)}, f32[1,512]{1,0:T(1,128)}) custom-call(bf16[20,64,640]{2,1,0:T(8,128)(2,1)} %bitcast.10, bf16[20,64,640]{2,1,0:T(8,128)(2,1)} %bitcast.11, bf16[20,640,256]{2,1,0:T(8,128)(2,1)} %leg_hbm.1, bf16[2,1280,640]{2,1,0:T(8,128)(2,1)} %constant.3.clone.tab_hbm, f32[1,256]{1,0:T(1,128)} %bitcast.14, ...), custom_call_target="tpu_custom_call" | custom-call | tf_op jit(solution)/shard_map/pallas_call | solution.py:490
  96.8 1.3 %broadcast_multiply_fusion = f32[1,512]{1,0:T(1,128)} fusion(f32[1,512]{1,0:T(1,128)} %get-tuple-element.9), kind=kLoop, calls=%fused_computation.2 | loop fusion | flops 512 | bytes 4096 | tf_op jit(solution)/shard_map/mul | solution.py:515
  98.1 1.5 %slice_multiply_fusion = (f32[32,512]{1,0:T(8,128)}, f32[512,32]{0,1:T(8,128)}) fusion(f32[64,512]{1,0:T(8,128)} %get-tuple-element.8), kind=kLoop, calls=%fused_computation | loop fusion | flops 32768 | bytes 262144 | tf_op jit(solution)/shard_map/mul | solution.py:515
  99.6 4.0 %copy.16 = f32[1,20,64,640]{3,2,1,0:T(8,128)} copy(f32[1,20,64,640]{3,2,1,0:T(8,128)} %bitcast.9) | data formatting | bytes 6553600

commit v2 on v1

--- a/solution.py
+++ b/solution.py
@@ -26,9 +26,12 @@
 HID = 512
 COLS = 640
 JT = 640
-SEND = ((0, 48), (48, 80), (80, 128), (128, 160))
+SEND = ((0, 16), (16, 32), (32, 48), (48, 80), (80, 128), (128, 160))
+ARRIVE = ((0, 1, 2), (3,), (4,), (5,))
 BACK = ((0, 32), (32, 48), (48, 80))
 GR = 17
+STEP = 4
+VMEM_LIMIT = 44 * 2**20
 
 
 def table_rows(e):
@@ -57,12 +60,42 @@
     return lax.dot_general(a, b, (((ca,), (cb,)), ((), ())), preferred_element_type=F32)
 
 
+def implicit_factor(damping):
+    across = lax.broadcasted_iota(jnp.int32, (CH, CH), 0)
+    along = lax.broadcasted_iota(jnp.int32, (CH, CH), 1)
+    column = jnp.sum(jnp.where(across == along, damping, 0.0), axis=1, keepdims=True)
+    degree = lax.broadcasted_iota(jnp.int32, (CH, NL), 1).astype(F32)
+    ratio = degree * (degree + 1.0) / (NL * (NL + 1.0))
+    return 1.0 / (1.0 + column * ratio)
+
+
+def inverse_kernel(a_ref, cot_ref, leg_ref, damp_ref, gr_ref, out_ref, gi_ref, gb_ref, go_ref, fac):
+    @pl.when(pl.program_id(0) == 0)
+    def _():
+        factor = implicit_factor(damp_ref[...])
+        fac[...] = jnp.concatenate([factor, factor], axis=0)
+        scale = 1.0 / math.sqrt(GRP * NP * NLON)
+        for e in range(XY):
+            block, tile = e // 4, e % 4
+            cols = pl.ds(128 * tile, 128)
+            piece = gr_ref[e, pl.ds(0, 16), :] * scale
+            if block < 2:
+                gi_ref[pl.ds(16 * block, 16), cols] = piece
+            else:
+                go_ref[pl.ds(16 * (block - 2), 16), cols] = piece
+            if block == 0:
+                gb_ref[:, cols] = gr_ref[e, pl.ds(16, 1), :] * scale
+
+    for i in range(STEP):
+        out_ref[i] = cot_ref[i].astype(F32) * fac[...] + dot(a_ref[i], leg_ref[i], 1, 1)
+
+
 def kernel(
     spec_hbm, cot_hbm, leg_hbm, tab_hbm, quad_ref, damp_ref, pin_ref, bias_ref, pout_ref,
-    out_hbm, og_ref, ob_ref,
-    spec, cot, leg, tab, factor, ft, stage, snd, rcv, rf, wdft, wp, w1t, racc, rall, bsnd, brcv,
-    gp, ga, gsnd, g1, g2s, g2r, g3s, g3r, g4s, g4r, outb,
-    in_sem, tab_sem, f_s, f_r, b_s, b_r, g_s, g_r, out_sem,
+    a_ref, gr_ref,
+    spec, cot, leg, tab, factor, ft, stage, snd, rcv, rf, wdft, wp, racc, rall, bsnd, brcv,
+    gp, ga, gsnd, g1, g2s, g2r, g3s, g3r, g4s, g4r,
+    in_sem, tab_sem, f_s, f_r, b_s, b_r, g_s, g_r,
 ):
     me = lax.axis_index("lat")
     grp = lax.axis_index("grp")
@@ -101,12 +134,9 @@
     tab_copy = pltpu.make_async_copy(tab_hbm, tab, tab_sem)
     tab_copy.start()
 
-    degree = lax.broadcasted_iota(jnp.int32, (CH, NL), 1).astype(F32)
-    ratio = degree * (degree + 1.0) / (NL * (NL + 1.0))
-    factor[...] = 1.0 / (1.0 + damp_ref[...] * ratio)
-
-    @pl.loop(0, MB)
-    def _(mm):
+    factor[...] = implicit_factor(damp_ref[...])
+
+    def legendre(mm):
         m = wave(mm)
         for copy in loads(mm):
             copy.wait()
@@ -123,29 +153,43 @@
         )
         ft[pl.ds(pl.multiple_of(mm * NP, NP), NP), :] = four.T
 
-    pl.semaphore_wait(barrier, LAT - 1 + GRP - 1)
-
-    def assemble(pair, d):
+    def tile(q, t, d):
+        rows = [
+            ft[pl.ds(8 * t * NP + 128 * half + 32 * q + d, 8, stride=NP), :] for half in range(2)
+        ]
+        return jnp.concatenate(rows, axis=0).astype(BF16)
+
+    def rest(pair, d):
         for j in range(4):
-            row = 128 * (j % 2) + 32 * (2 * pair + j // 2) + d
-            stage[pl.ds(MB * j, MB), :] = ft[pl.ds(row, MB, stride=NP), :]
-        snd[d, pl.ds(80 * pair, 80), :] = stage[...].astype(BF16)
-
-    def send(c, d):
-        lo, hi = SEND[c]
+            row = 16 * NP + 128 * (j % 2) + 32 * (2 * pair + j // 2) + d
+            stage[pl.ds(4 * j, 4), :] = ft[pl.ds(row, 4, stride=NP), :]
+        return stage[pl.ds(0, 16), :].astype(BF16)
+
+    def assemble(n, d):
+        if n < 2:
+            snd[d, pl.ds(16 * n, 16), :] = tile(0, n, d)
+        elif n == 2:
+            snd[d, pl.ds(32, 16), :] = rest(0, d)
+        elif n == 3:
+            for t in range(2):
+                snd[d, pl.ds(48 + 16 * t, 16), :] = tile(1, t, d)
+        elif n == 4:
+            for t in range(2):
+                snd[d, pl.ds(80 + 16 * t, 16), :] = tile(2, t, d)
+            snd[d, pl.ds(112, 16), :] = rest(1, d)
+        else:
+            for t in range(2):
+                snd[d, pl.ds(128 + 16 * t, 16), :] = tile(3, t, d)
+
+    def send(n, d):
+        lo, hi = SEND[n]
         pltpu.make_async_remote_copy(
             src_ref=snd.at[d, pl.ds(lo, hi - lo)],
             dst_ref=rcv.at[me, pl.ds(lo, hi - lo)],
-            send_sem=f_s.at[c],
-            recv_sem=f_r.at[c],
+            send_sem=f_s.at[n],
+            recv_sem=f_r.at[n],
             device_id={"lat": d},
             device_id_type=MESH,
-        ).start()
-
-    def keep(c):
-        lo, hi = SEND[c]
-        pltpu.make_async_copy(
-            snd.at[me, pl.ds(lo, hi - lo)], rcv.at[me, pl.ds(lo, hi - lo)], f_r.at[c]
         ).start()
 
     def far_then_near(f):
@@ -157,27 +201,36 @@
         def _(i):
             f(peer(2 * i))
 
-    def pack_send(pair, c):
+    def forward(n, ready=False):
         def f(d):
-            assemble(pair, d)
-            send(c, d)
-
-        return f
-
-    far_then_near(pack_send(0, 0))
-    assemble(0, me)
-    keep(0)
-    far_then_near(functools.partial(send, 1))
-    keep(1)
+            if not ready:
+                assemble(n, d)
+            send(n, d)
+
+        far_then_near(f)
+        if not ready:
+            assemble(n, me)
+        lo, hi = SEND[n]
+        pltpu.make_async_copy(
+            snd.at[me, pl.ds(lo, hi - lo)], rcv.at[me, pl.ds(lo, hi - lo)], f_r.at[n]
+        ).start()
+
+    pl.loop(0, 8)(legendre)
+    pl.semaphore_wait(barrier, LAT - 1 + GRP - 1)
+    forward(0)
+    pl.loop(8, 16)(legendre)
+    forward(1)
+    pl.loop(16, MB)(legendre)
+    forward(2)
+    forward(3)
 
     @pl.loop(0, LAT)
     def _(d):
-        assemble(1, d)
+        assemble(4, d)
+        assemble(5, d)
 
     wp[...] = jnp.zeros_like(wp)
-    w_in = pin_ref[...].astype(F32).T
-    w1t[...] = w_in.astype(BF16)
-    half_in = (0.5 * w_in).astype(BF16)
+    half_in = (0.5 * pin_ref[...].astype(F32)).astype(BF16)
     half_out = (0.5 * pout_ref[...].astype(F32)).astype(BF16)
     half_bias = 0.5 * bias_ref[...]
     top = half_bias.astype(BF16).astype(F32)
@@ -199,22 +252,26 @@
     left = lane < 64
 
     def arrive(c):
-        lo, hi = SEND[c]
-        span = rcv.at[:, pl.ds(lo, hi - lo)]
-        pltpu.make_async_copy(span, span, f_r.at[c]).wait()
-
-        at = lo % 80
-
-        @pl.loop(0, LAT)
-        def _(src):
-            rf[pl.ds(pl.multiple_of(src * 80 + at, 8), hi - lo), :] = rcv[
-                src, pl.ds(lo, hi - lo), :
-            ].astype(F32)
-
-        first = 40 * (c % 2)
+        for n in ARRIVE[c]:
+            lo, hi = SEND[n]
+            span = rcv.at[:, pl.ds(lo, hi - lo)]
+            pltpu.make_async_copy(span, span, f_r.at[n]).wait()
+            at = lo % 80
+
+            @pl.loop(0, LAT)
+            def _(src):
+                rf[pl.ds(pl.multiple_of(src * 80 + at, 8), hi - lo), :] = rcv[
+                    src, pl.ds(lo, hi - lo), :
+                ].astype(F32)
+
+        def row(half, mm):
+            if mm < 16:
+                return 48 * (c % 2) + 16 * (mm // 8) + 8 * half + mm % 8
+            return 32 + 8 * (c % 2) + 4 * half + mm - 16
+
         for mm in range(MB):
-            w0 = rf[pl.ds(first + mm, LAT, stride=80), :]
-            w1 = rf[pl.ds(first + MB + mm, LAT, stride=80), :]
+            w0 = rf[pl.ds(row(0, mm), LAT, stride=80), :]
+            w1 = rf[pl.ds(row(1, mm), LAT, stride=80), :]
             re = jnp.where(left, w0, pltpu.roll(w1, 64, 1))
             im = jnp.where(left, pltpu.roll(w0, 64, 1), w1)
             r_re, r_im = table_rows(mm % HB)
@@ -240,7 +297,7 @@
             act = h * a
             pre = (u * (a * ((1.0 + (h + h)) - act))).astype(BF16)
             act = act.astype(BF16)
-            grads.append(dot(w1t[...], pre, 1, 1))
+            grads.append(dot(pin_ref[...], pre, 1, 1))
             lhs = jnp.concatenate([xt[64 * s : 64 * s + CH], ones_t], axis=0)
             gp[...] += dot(lhs, pre, 1, 0)
             ga[...] += dot(xt[64 * s + CH : 64 * s + 64], act, 1, 0)
@@ -359,12 +416,7 @@
 
     def reduce_5():
         pltpu.make_async_copy(g4r, g4r, g_r.at[3]).wait()
-        for e in range(XY):
-            block, tile = e // 4, e % 4
-            cols = pl.ds(128 * tile, 128)
-            og_ref[pl.ds(16 * block, 16), cols] = g4r[e, pl.ds(0, 16), :]
-            if block == 0:
-                ob_ref[:, cols] = g4r[e, pl.ds(16, 1), :]
+        gr_ref[...] = g4r[...]
 
     @pl.loop(0, 4)
     def _(c):
@@ -374,8 +426,7 @@
             def _():
                 arrive(now)
                 if now < 2:
-                    far_then_near(functools.partial(send, now + 2))
-                    keep(now + 2)
+                    forward(now + 4, ready=True)
 
         racc[...] = jnp.zeros_like(racc)
         lax.fori_loop(0, HALF // JT, physics, 0)
@@ -400,38 +451,34 @@
                 src, pl.ds(lo, hi - lo), :
             ].astype(F32)
 
-    def inverse(mm, _):
-        m = wave(mm)
-        rows = jnp.concatenate(
-            [rf[pl.ds(MB * q + mm, LAT, stride=80), :] for q in range(4)], axis=0
-        )
-        t = rows.T.astype(BF16)
-        lhs = jnp.concatenate(
-            [
-                jnp.concatenate([t[:32], t[64:96]], axis=0),
-                jnp.concatenate([t[32:64], t[96:]], axis=0),
-            ],
-            axis=1,
-        )
-        fac = factor[...]
-        direct = cot[m].astype(F32) * jnp.concatenate([fac, fac], axis=0)
-        outb[m] = direct + dot(lhs, leg[m], 1, 1)
-        pltpu.make_async_copy(outb.at[m], out_hbm.at[m], out_sem).start()
-        return 0
-
+    reduce_2()
     unpack(0)
+    reduce_3()
     unpack(1)
-    reduce_2()
-    reduce_3()
+    reduce_4()
     unpack(2)
-    reduce_4()
-    lax.fori_loop(0, MB, inverse, 0)
+
+    @pl.loop(0, MB // 4)
+    def _(step):
+        for sub in range(4):
+            mm = 4 * step + sub
+            rows = jnp.concatenate(
+                [rf[pl.ds(MB * q + mm, LAT, stride=80), :] for q in range(4)], axis=0
+            )
+            t = rows.T.astype(BF16)
+            a_ref[wave(mm)] = jnp.concatenate(
+                [
+                    jnp.concatenate([t[:32], t[64:96]], axis=0),
+                    jnp.concatenate([t[32:64], t[96:]], axis=0),
+                ],
+                axis=1,
+            )
+
     reduce_5()
 
-    pltpu.make_async_copy(outb, out_hbm, out_sem).wait()
-    for c, (lo, hi) in enumerate(SEND):
+    for n, (lo, hi) in enumerate(SEND):
         span = snd.at[pl.ds(0, LAT - 1), pl.ds(lo, hi - lo)]
-        pltpu.make_async_copy(span, span, f_s.at[c]).wait()
+        pltpu.make_async_copy(span, span, f_s.at[n]).wait()
     for n, (lo, hi) in enumerate(BACK):
         span = bsnd.at[pl.ds(0, LAT - 1), pl.ds(lo, hi - lo)]
         pltpu.make_async_copy(span, span, b_s.at[n]).wait()
@@ -461,7 +508,6 @@
         pltpu.VMEM((LAT * 80, 128), F32),
         pltpu.VMEM((2, COLS, 128), BF16),
         pltpu.VMEM((2, 256, 2 * HID), BF16),
-        pltpu.VMEM((CH, HID), BF16),
         pltpu.VMEM((2, 64, COLS), F32),
         pltpu.VMEM((4 * 640, 128), F32),
         pltpu.VMEM((LAT, 80, 128), BF16),
@@ -476,29 +522,26 @@
         pltpu.VMEM((GRP, GR, 128), F32),
         pltpu.VMEM((GR, 128), F32),
         pltpu.VMEM((XY, GR, 128), F32),
-        pltpu.VMEM((MB, 2 * CH, NL), F32),
         dma((3, MB)),
         dma,
-        dma((4,)),
-        dma((4,)),
+        dma((6,)),
+        dma((6,)),
         dma((3,)),
         dma((3,)),
         dma((4,)),
         dma((4,)),
-        dma,
     ]
-    grad_state, grads, grad_bias = pl.pallas_call(
+    fourier, grads = pl.pallas_call(
         kernel,
         out_shape=[
-            jax.ShapeDtypeStruct((MB, 2 * CH, NL), F32),
-            jax.ShapeDtypeStruct((2 * CH, HID), F32),
-            jax.ShapeDtypeStruct((1, HID), F32),
+            jax.ShapeDtypeStruct((MB, 2 * CH, NP), BF16),
+            jax.ShapeDtypeStruct((XY, GR, 128), F32),
         ],
         in_specs=[hbm] * 4 + [vmem] * 5,
-        out_specs=[hbm, vmem, vmem],
+        out_specs=[vmem, vmem],
         scratch_shapes=scratch,
         compiler_params=pltpu.CompilerParams(
-            collective_id=0, has_side_effects=True, vmem_limit_bytes=60 * 2**20
+            collective_id=0, has_side_effects=True, vmem_limit_bytes=VMEM_LIMIT
         ),
     )(
         spectral_state[0],
@@ -506,13 +549,34 @@
         legendre,
         tables,
         quadrature[None, :],
-        damping[:, None],
-        physics_in,
+        damping[None, :],
+        physics_in.T,
         physics_bias[None, :],
         physics_out,
     )
-    scale = 1.0 / math.sqrt(GRP * NP * NLON)
-    return (grad_state[None], grads[:CH].T * scale, grad_bias[0] * scale, grads[CH:] * scale)
+    whole = lambda *shape: pl.BlockSpec(shape, lambda i: (0,) * len(shape))
+    part = lambda *shape: pl.BlockSpec((STEP,) + shape, lambda i: (i, 0, 0))
+    grad_state, grad_in, grad_bias, grad_out = pl.pallas_call(
+        inverse_kernel,
+        grid=(MB // STEP,),
+        out_shape=[
+            jax.ShapeDtypeStruct((MB, 2 * CH, NL), F32),
+            jax.ShapeDtypeStruct((CH, HID), F32),
+            jax.ShapeDtypeStruct((1, HID), F32),
+            jax.ShapeDtypeStruct((CH, HID), F32),
+        ],
+        in_specs=[
+            part(2 * CH, NP),
+            part(2 * CH, NL),
+            part(NL, NP),
+            whole(1, CH),
+            whole(XY, GR, 128),
+        ],
+        out_specs=[part(2 * CH, NL), whole(CH, HID), whole(1, HID), whole(CH, HID)],
+        scratch_shapes=[pltpu.VMEM((2 * CH, NL), F32)],
+        compiler_params=pltpu.CompilerParams(vmem_limit_bytes=24 * 2**20),
+    )(fourier, cotangent[0], legendre, damping[None, :], grads)
+    return (grad_state[None], grad_in.T, grad_bias[0], grad_out)
 
 
 def solution(mesh):

time: 104 us -> 104 us (level)
  other arithmetic: 2.79 us -> 0.01 us
  local copies, waits for them, and re-layouts: 6.82 us -> 8.63 us
    unnamed x2 -> x20, local copies, waits for them, and re-layouts: 5.48 us -> 8.63 us
    mul x2 -> x0, other arithmetic: 2.79 us -> none  [the longest x1 1.53 us: body(): grads[CH:] * scale]
    broadcast_in_dim x1 -> x0, local copies, waits for them, and re-layouts: 1.34 us -> none  [body(): damping[:, None]]
    pallas_call x1 -> x2, Pallas kernels: 93.3 us -> 94.1 us  [the longest x1 89.9 us: body(): pl.pallas_call(kernel, out_shape=[jax.ShapeDtypeStruct((MB, 2 * CH, NP),...]
where the time goes in v2:
time: 104 us; the launch traced here: 103 us
  Pallas kernels  94.1 us (90%)
  local copies, waits for them, and re-layouts  8.63 us (8%)
    pallas_call x1, Pallas kernels, body(): pl.pallas_call(kernel, out_shape=[jax.ShapeDtypeStruct((MB, 2 * CH, NP),...  89.9 us
    unnamed x20, local copies, waits for them, and re-layouts  8.63 us
    pallas_call x1, Pallas kernels, body(): pl.pallas_call(inverse_kernel, grid=(MB // STEP,), out_shape=[jax.ShapeDt...  4.17 us

profile of v2, /device:TPU:1, one launch (start us, length us, event | category | flops | bytes accessed | tf_op | source)
XLA Modules:
  0.0 103.4 jit_solution(12871563475451515325)
XLA Ops:
  0.6 0.0 slice-start
  0.6 0.0 copy-start
  0.7 1.6 %copy-done = bf16[1,20,64,640]{3,2,1,0:T(8,128)(2,1)S(1)} copy-done((bf16[1,20,64,640]{3,2,1,0:T(8,128)(2,1)S(1)}, bf16[1,20,64,640]{3,2,1,0:T(8,128)(2,1)}, u32[]{:S(2)}) %copy-start) | copy-done | bytes 1638424
  2.2 0.0 copy-start.1
  2.2 2.1 %copy-done.1 = bf16[2,1280,640]{2,1,0:T(8,128)(2,1)S(1)} copy-done((bf16[2,1280,640]{2,1,0:T(8,128)(2,1)S(1)}, bf16[2,1280,640]{2,1,0:T(8,128)(2,1)}, u32[]{:S(2)}) %copy-start.1) | copy-done | bytes 3276824
  4.3 0.0 copy-start.2
  4.3 1.4 %copy-done.2 = bf16[1,20,64,640]{3,2,1,0:T(8,128)(2,1)S(1)} copy-done((bf16[1,20,64,640]{3,2,1,0:T(8,128)(2,1)S(1)}, bf16[1,20,64,640]{3,2,1,0:T(8,128)(2,1)}, u32[]{:S(2)}) %copy-start.2) | copy-done | bytes 1638424
  5.7 0.0 copy-start.3
  5.7 0.8 copy-done.3
  6.5 0.0 copy-start.4
  6.5 0.8 copy-done.4
  7.3 0.0 copy-start.5
  7.3 0.7 copy-done.5
  7.9 0.0 copy-start.6
  7.9 0.7 copy-done.6
  8.6 0.0 copy-start.7
  8.6 0.7 copy-done.7
  9.3 0.0 slice-start.1
  9.3 89.9 %shard_map.120 = (bf16[20,64,256]{2,1,0:T(8,128)(2,1)S(1)}, f32[16,17,128]{2,1,0:T(8,128)S(1)}) custom-call(bf16[20,64,640]{2,1,0:T(8,128)(2,1)S(1)} %bitcast.13, bf16[20,64,640]{2,1,0:T(8,128)(2,1)S(1)} %bitcast.11, bf16[20,640,256]{2,1,0:T(8,128)(2,1)} %leg_ref.1, bf16[2,1280,640]{2,1,0:T(8,128)(2,1)S(1)} %copy-done.1, f32[1,256]{1,0:T(1,128)S(1)} %bitcast.18, ...), custom_call_target="tpu_custom_call" | custom-call | tf_op jit(solution)/shard_map/pallas_call | solution.py:534
  99.2 0.0 slice-done
  99.2 0.0 slice-done.1
  99.2 4.2 %shard_map.121 = (f32[20,64,640]{2,1,0:T(8,128)}, f32[32,512]{1,0:T(8,128)}, f32[1,512]{1,0:T(1,128)}, f32[32,512]{1,0:T(8,128)}) custom-call(bf16[20,64,256]{2,1,0:T(8,128)(2,1)S(1)} %get-tuple-element.10.a_ref, bf16[20,64,640]{2,1,0:T(8,128)(2,1)S(1)} %bitcast.12, bf16[20,640,256]{2,1,0:T(8,128)(2,1)S(1)} %bitcast.10, f32[1,32]{1,0:T(1,128)S(1)} %bitcast.17, ...), custom_call_target="tpu_custom_call" | custom-call | tf_op jit(solution)/shard_map/pallas_call | solution.py:559
  (1 shorter events, 0.0 us)
Async XLA Ops:
  0.6 98.6 %slice-start = ((s8[6553600]{0:T(1024)(128)(4,1)}), s8[4194304]{0:T(1024)(128)(4,1)S(1)}, s32[]{:S(2)}) async-start(s8[6553600]{0:T(1024)(128)(4,1)} %bitcast.9), calls=%async_computation | async-start | bytes 8388608
  0.6 1.6 %copy-start = (bf16[1,20,64,640]{3,2,1,0:T(8,128)(2,1)S(1)}, bf16[1,20,64,640]{3,2,1,0:T(8,128)(2,1)}, u32[]{:S(2)}) copy-start(bf16[1,20,64,640]{3,2,1,0:T(8,128)(2,1)} %param.10) | copy-start | bytes 4915204
  2.2 2.1 %copy-start.1 = (bf16[2,1280,640]{2,1,0:T(8,128)(2,1)S(1)}, bf16[2,1280,640]{2,1,0:T(8,128)(2,1)}, u32[]{:S(2)}) copy-start(bf16[2,1280,640]{2,1,0:T(8,128)(2,1)} %constant.2.clone.tab_hbm) | copy-start | bytes 9830404
  4.3 1.4 %copy-start.2 = (bf16[1,20,64,640]{3,2,1,0:T(8,128)(2,1)S(1)}, bf16[1,20,64,640]{3,2,1,0:T(8,128)(2,1)}, u32[]{:S(2)}) copy-start(bf16[1,20,64,640]{3,2,1,0:T(8,128)(2,1)} %param.9) | copy-start | bytes 4915204
  5.7 0.8 copy-start.3
  6.5 0.8 copy-start.4
  7.3 0.7 copy-start.5
  7.9 0.7 copy-start.6
  8.6 0.7 copy-start.7
  9.3 90.0 %slice-start.1 = ((s8[6553600]{0:T(1024)(128)(4,1)}), s8[2359296]{0:T(1024)(128)(4,1)S(1)}, s32[]{:S(2)}) async-start(s8[6553600]{0:T(1024)(128)(4,1)} %bitcast.9), calls=%async_computation.1 | async-start | bytes 4718592

commit v3 on v2

--- a/solution.py
+++ b/solution.py
@@ -31,7 +31,7 @@
 BACK = ((0, 32), (32, 48), (48, 80))
 GR = 17
 STEP = 4
-VMEM_LIMIT = 44 * 2**20
+VMEM_LIMIT = 54 * 2**20
 
 
 def table_rows(e):
@@ -91,15 +91,16 @@
 
 
 def kernel(
-    spec_hbm, cot_hbm, leg_hbm, tab_hbm, quad_ref, damp_ref, pin_ref, bias_ref, pout_ref,
+    spec_hbm, cot_hbm, leg_hbm, tab_hbm, quad_hbm, damp_hbm, pin_hbm, bias_hbm, pout_hbm,
     a_ref, gr_ref,
-    spec, cot, leg, tab, factor, ft, stage, snd, rcv, rf, wdft, wp, racc, rall, bsnd, brcv,
-    gp, ga, gsnd, g1, g2s, g2r, g3s, g3r, g4s, g4r,
-    in_sem, tab_sem, f_s, f_r, b_s, b_r, g_s, g_r,
+    quad_ref, damp_ref, pin_ref, bias_ref, pout_ref, spec, cot, leg, tab, factor, ft, stage, snd, rcv, rf, wdft, wp, held, racc, rall, bsnd, brcv,
+    gp, ga, gsnd, g1, g2s, g2r, g3s, g3r,
+    small_sem, in_sem, tab_sem, f_s, f_r, b_s, b_r, g_s, g_r,
 ):
     me = lax.axis_index("lat")
     grp = lax.axis_index("grp")
     xy = me // 2
+    partner = me + 1 - 2 * lax.rem(me, 2)
 
     def peer(k):
         return lax.rem(me + k, LAT)
@@ -114,6 +115,15 @@
     def _(k):
         pl.semaphore_signal(
             barrier, inc=1, device_id={"grp": lax.rem(grp + k, GRP)}, device_id_type=MESH
+        )
+
+    @pl.loop(1, GRP)
+    def _(k):
+        pl.semaphore_signal(
+            barrier,
+            inc=1,
+            device_id={"lat": partner, "grp": lax.rem(grp + k, GRP)},
+            device_id_type=MESH,
         )
 
     def wave(mm):
@@ -126,6 +136,21 @@
             for i, (src, dst) in enumerate(((spec_hbm, spec), (cot_hbm, cot), (leg_hbm, leg)))
         ]
 
+    small = [
+        pltpu.make_async_copy(src, dst, small_sem.at[i])
+        for i, (src, dst) in enumerate(
+            (
+                (damp_hbm, damp_ref),
+                (quad_hbm, quad_ref),
+                (pin_hbm, pin_ref),
+                (bias_hbm, bias_ref),
+                (pout_hbm, pout_ref),
+            )
+        )
+    ]
+    for copy in small:
+        copy.start()
+
     @pl.loop(0, MB)
     def _(mm):
         for copy in loads(mm):
@@ -134,6 +159,8 @@
     tab_copy = pltpu.make_async_copy(tab_hbm, tab, tab_sem)
     tab_copy.start()
 
+    for copy in small:
+        copy.wait()
     factor[...] = implicit_factor(damp_ref[...])
 
     def legendre(mm):
@@ -216,7 +243,7 @@
         ).start()
 
     pl.loop(0, 8)(legendre)
-    pl.semaphore_wait(barrier, LAT - 1 + GRP - 1)
+    pl.semaphore_wait(barrier, LAT - 1 + 2 * (GRP - 1))
     forward(0)
     pl.loop(8, 16)(legendre)
     forward(1)
@@ -282,7 +309,7 @@
     ones = jnp.where(one_lane < 3, 1.0, 0.0).astype(BF16)
     ones_t = jnp.ones((16, 2 * JT), BF16)
 
-    def physics(i, _):
+    def columns(i, grid_gradient):
         span = pl.ds(pl.multiple_of(i * JT, JT), JT)
         even = dot(tab[0, span, :], wdft[0], 1, 0)
         odd = dot(tab[1, span, :], wdft[1], 1, 0)
@@ -297,16 +324,31 @@
             act = h * a
             pre = (u * (a * ((1.0 + (h + h)) - act))).astype(BF16)
             act = act.astype(BF16)
-            grads.append(dot(pin_ref[...], pre, 1, 1))
+            grads.append(grid_gradient(s, pre))
             lhs = jnp.concatenate([xt[64 * s : 64 * s + CH], ones_t], axis=0)
             gp[...] += dot(lhs, pre, 1, 0)
             ga[...] += dot(xt[64 * s + CH : 64 * s + 64], act, 1, 0)
+        return grads
+
+    def longitudes(i, grads):
+        span = pl.ds(pl.multiple_of(i * JT, JT), JT)
         gg = jnp.concatenate(grads, axis=0)
         g_even = (gg[:, :JT] + gg[:, JT:]).astype(BF16)
         g_odd = (gg[:, :JT] - gg[:, JT:]).astype(BF16)
         racc[0] += dot(g_even, tab[0, span, :], 1, 0)
         racc[1] += dot(g_odd, tab[1, span, :], 1, 0)
-        return 0
+
+    def physics(i):
+        longitudes(i, columns(i, lambda s, pre: dot(pin_ref[...], pre, 1, 1)))
+
+    def hold(i):
+        def keep(s, pre):
+            held[i, s] = pre
+
+        columns(i, keep)
+
+    def finish(i):
+        longitudes(i, [dot(pin_ref[...], held[i, s], 1, 1) for s in range(2)])
 
     def turn(c):
         for parity in range(2):
@@ -320,18 +362,18 @@
             both = jnp.concatenate([last, pltpu.roll(last, 64, 1)], axis=0).T
             rall[pl.ds(base + 256, 64), :] = both[:64]
 
-    def back(n):
+    def pack(n, d):
         lo, hi = BACK[n]
-        first = lo // MB
-        last = (hi - 1) // MB
-
-        def pack(d):
-            for q in range(first, last + 1):
-                stage[pl.ds(MB * q, MB), :] = rall[pl.ds(640 * q + d, MB, stride=LAT), :]
-            bsnd[d, pl.ds(lo, hi - lo), :] = stage[pl.ds(lo, hi - lo), :].astype(BF16)
+        for q in range(lo // MB, (hi - 1) // MB + 1):
+            stage[pl.ds(MB * q, MB), :] = rall[pl.ds(640 * q + d, MB, stride=LAT), :]
+        bsnd[d, pl.ds(lo, hi - lo), :] = stage[pl.ds(lo, hi - lo), :].astype(BF16)
+
+    def back(n, ready=False):
+        lo, hi = BACK[n]
 
         def go(d):
-            pack(d)
+            if not ready:
+                pack(n, d)
             pltpu.make_async_remote_copy(
                 src_ref=bsnd.at[d, pl.ds(lo, hi - lo)],
                 dst_ref=brcv.at[me, pl.ds(lo, hi - lo)],
@@ -342,7 +384,8 @@
             ).start()
 
         far_then_near(go)
-        pack(me)
+        if not ready:
+            pack(n, me)
         pltpu.make_async_copy(
             bsnd.at[me, pl.ds(lo, hi - lo)], brcv.at[me, pl.ds(lo, hi - lo)], b_r.at[n]
         ).start()
@@ -379,44 +422,36 @@
         for e in range(1, XY):
             total = total + g1[e]
         g2s[...] = total
-        copy = pltpu.make_async_remote_copy(
-            src_ref=g2s,
-            dst_ref=g2r,
-            send_sem=g_s.at[1],
-            recv_sem=g_r.at[1],
-            device_id={"lat": me + 1 - 2 * lax.rem(me, 2)},
-            device_id_type=MESH,
-        )
-        copy.start()
+
+        for far in (1, 0):
+
+            @pl.loop(1 - far, GRP)
+            def _(k):
+                pltpu.make_async_remote_copy(
+                    src_ref=g2s,
+                    dst_ref=g2r.at[GRP * lax.rem(me, 2) + grp],
+                    send_sem=g_s.at[1],
+                    recv_sem=g_r.at[1],
+                    device_id={
+                        "lat": partner if far else me,
+                        "grp": lax.rem(grp + k, GRP),
+                    },
+                    device_id_type=MESH,
+                ).start()
+
+        pltpu.make_async_copy(g2s, g2r.at[GRP * lax.rem(me, 2) + grp], g_r.at[1]).start()
 
     def reduce_3():
         pltpu.make_async_copy(g2r, g2r, g_r.at[1]).wait()
-        g3s[...] = g2s[...] + g2r[...]
-
-        @pl.loop(1, GRP)
-        def _(k):
-            pltpu.make_async_remote_copy(
-                src_ref=g3s,
-                dst_ref=g3r.at[grp],
-                send_sem=g_s.at[2],
-                recv_sem=g_r.at[2],
-                device_id={"grp": lax.rem(grp + k, GRP)},
-                device_id_type=MESH,
-            ).start()
-
-        pltpu.make_async_copy(g3s, g3r.at[grp], g_r.at[2]).start()
+        total = g2r[0]
+        for e in range(1, 2 * GRP):
+            total = total + g2r[e]
+        g3s[...] = total
+        xy_step(2, lambda e: g3s, g3r, xy)
 
     def reduce_4():
         pltpu.make_async_copy(g3r, g3r, g_r.at[2]).wait()
-        total = g3r[0]
-        for e in range(1, GRP):
-            total = total + g3r[e]
-        g4s[...] = total
-        xy_step(3, lambda e: g4s, g4r, xy)
-
-    def reduce_5():
-        pltpu.make_async_copy(g4r, g4r, g_r.at[3]).wait()
-        gr_ref[...] = g4r[...]
+        gr_ref[...] = g3r[...]
 
     @pl.loop(0, 4)
     def _(c):
@@ -429,16 +464,31 @@
                     forward(now + 4, ready=True)
 
         racc[...] = jnp.zeros_like(racc)
-        lax.fori_loop(0, HALF // JT, physics, 0)
+
+        @pl.when(c < 3)
+        def _():
+            pl.loop(0, HALF // JT)(physics)
+
+        @pl.when(c == 3)
+        def _():
+            pl.loop(0, HALF // JT)(hold)
+            reduce_1()
+            pl.loop(0, HALF // JT)(finish)
+
         for now in range(4):
 
             @pl.when(c == now)
             def _():
-                if now == 3:
-                    reduce_1()
                 turn(now)
-                if now > 0:
+                if now in (1, 2):
                     back(now - 1)
+
+    @pl.loop(0, LAT)
+    def _(d):
+        pack(2, d)
+
+    reduce_2()
+    back(2, ready=True)
 
     def unpack(n):
         lo, hi = BACK[n]
@@ -451,11 +501,9 @@
                 src, pl.ds(lo, hi - lo), :
             ].astype(F32)
 
-    reduce_2()
     unpack(0)
+    unpack(1)
     reduce_3()
-    unpack(1)
-    reduce_4()
     unpack(2)
 
     @pl.loop(0, MB // 4)
@@ -474,7 +522,7 @@
                 axis=1,
             )
 
-    reduce_5()
+    reduce_4()
 
     for n, (lo, hi) in enumerate(SEND):
         span = snd.at[pl.ds(0, LAT - 1), pl.ds(lo, hi - lo)]
@@ -482,10 +530,9 @@
     for n, (lo, hi) in enumerate(BACK):
         span = bsnd.at[pl.ds(0, LAT - 1), pl.ds(lo, hi - lo)]
         pltpu.make_async_copy(span, span, b_s.at[n]).wait()
-    for n, count, buf in ((0, XY - 1, g1), (2, GRP - 1, g3r), (3, XY - 1, g4r)):
+    for n, count, buf in ((0, XY - 1, g1), (1, 2 * GRP - 1, g2r), (2, XY - 1, g3r)):
         span = buf.at[pl.ds(0, count)]
         pltpu.make_async_copy(span, span, g_s.at[n]).wait()
-    pltpu.make_async_copy(g2s, g2s, g_s.at[1]).wait()
 
 
 def body(
@@ -496,6 +543,11 @@
     vmem = pl.BlockSpec(memory_space=pltpu.VMEM)
     dma = pltpu.SemaphoreType.DMA
     scratch = [
+        pltpu.VMEM((1, NP), F32),
+        pltpu.VMEM((1, CH), F32),
+        pltpu.VMEM((CH, HID), BF16),
+        pltpu.VMEM((1, HID), F32),
+        pltpu.VMEM((CH, HID), BF16),
         pltpu.VMEM((MB, 2 * CH, NL), BF16),
         pltpu.VMEM((MB, 2 * CH, NL), BF16),
         pltpu.VMEM((MB, NL, NP), BF16),
@@ -508,6 +560,7 @@
         pltpu.VMEM((LAT * 80, 128), F32),
         pltpu.VMEM((2, COLS, 128), BF16),
         pltpu.VMEM((2, 256, 2 * HID), BF16),
+        pltpu.VMEM((HALF // JT, 2, 2 * JT, HID), BF16),
         pltpu.VMEM((2, 64, COLS), F32),
         pltpu.VMEM((4 * 640, 128), F32),
         pltpu.VMEM((LAT, 80, 128), BF16),
@@ -517,19 +570,18 @@
         pltpu.VMEM((XY, GR, 128), F32),
         pltpu.VMEM((XY, GR, 128), F32),
         pltpu.VMEM((GR, 128), F32),
-        pltpu.VMEM((GR, 128), F32),
-        pltpu.VMEM((GR, 128), F32),
-        pltpu.VMEM((GRP, GR, 128), F32),
+        pltpu.VMEM((2 * GRP, GR, 128), F32),
         pltpu.VMEM((GR, 128), F32),
         pltpu.VMEM((XY, GR, 128), F32),
+        dma((5,)),
         dma((3, MB)),
         dma,
         dma((6,)),
         dma((6,)),
         dma((3,)),
         dma((3,)),
-        dma((4,)),
-        dma((4,)),
+        dma((3,)),
+        dma((3,)),
     ]
     fourier, grads = pl.pallas_call(
         kernel,
@@ -537,7 +589,7 @@
             jax.ShapeDtypeStruct((MB, 2 * CH, NP), BF16),
             jax.ShapeDtypeStruct((XY, GR, 128), F32),
         ],
-        in_specs=[hbm] * 4 + [vmem] * 5,
+        in_specs=[hbm] * 9,
         out_specs=[vmem, vmem],
         scratch_shapes=scratch,
         compiler_params=pltpu.CompilerParams(

time: 104 us -> 93.3 us (0.90)
  local copies, waits for them, and re-layouts: 8.63 us -> 2.02 us
  Pallas kernels: 94.1 us -> 90.4 us
    unnamed x20 -> x12, local copies, waits for them, and re-layouts: 8.63 us -> 2.02 us
    pallas_call x1, Pallas kernels: 89.9 us -> 86.2 us  [body(): pl.pallas_call(kernel, out_shape=[jax.ShapeDtypeStruct((MB, 2 * CH, NP),...]
where the time goes in v3:
time: 93.3 us; the launch traced here: 93.1 us
  Pallas kernels  90.4 us (97%)
  local copies, waits for them, and re-layouts  2.02 us (2%)
    pallas_call x1, Pallas kernels, body(): pl.pallas_call(kernel, out_shape=[jax.ShapeDtypeStruct((MB, 2 * CH, NP),...  86.2 us
    pallas_call x1, Pallas kernels, body(): pl.pallas_call(inverse_kernel, grid=(MB // STEP,), out_shape=[jax.ShapeDt...  4.15 us
    unnamed x12, local copies, waits for them, and re-layouts  2.02 us

profile of v3, /device:TPU:1, one launch (start us, length us, event | category | flops | bytes accessed | tf_op | source)
XLA Modules:
  0.0 93.1 jit_solution(10581832228728929953)
XLA Ops:
  0.6 0.0 slice-start
  0.6 0.0 slice-start.1
  0.7 0.0 copy-start
  0.7 0.0 copy-start.3
  0.7 86.2 %shard_map.120 = (bf16[20,64,256]{2,1,0:T(8,128)(2,1)}, f32[16,17,128]{2,1,0:T(8,128)}) custom-call(bf16[20,64,640]{2,1,0:T(8,128)(2,1)} %bitcast.15, bf16[20,64,640]{2,1,0:T(8,128)(2,1)} %bitcast.11, bf16[20,640,256]{2,1,0:T(8,128)(2,1)} %leg_ref.1, bf16[2,1280,640]{2,1,0:T(8,128)(2,1)} %constant.2.clone.tab_hbm, f32[1,256]{1,0:T(1,128)} %bitcast.18, ...), custom_call_target="tpu_custom_call" | custom-call | tf_op jit(solution)/shard_map/pallas_call | solution.py:586
  86.9 0.0 slice-done
  86.9 0.0 slice-done.1
  86.9 0.0 copy-done
  86.9 0.0 copy-done.3
  86.9 0.0 copy-start.1
  87.0 1.1 %copy-done.1 = bf16[20,64,256]{2,1,0:T(8,128)(2,1)S(1)} copy-done((bf16[20,64,256]{2,1,0:T(8,128)(2,1)S(1)}, bf16[20,64,256]{2,1,0:T(8,128)(2,1)}, u32[]{:S(2)}) %copy-start.1) | copy-done | bytes 655384
  88.0 0.0 copy-start.2
  88.0 0.9 copy-done.2
  89.0 4.1 %shard_map.121 = (f32[20,64,640]{2,1,0:T(8,128)}, f32[32,512]{1,0:T(8,128)}, f32[1,512]{1,0:T(1,128)}, f32[32,512]{1,0:T(8,128)}) custom-call(bf16[20,64,256]{2,1,0:T(8,128)(2,1)S(1)} %copy-done.1, bf16[20,64,640]{2,1,0:T(8,128)(2,1)S(1)} %bitcast.12, bf16[20,640,256]{2,1,0:T(8,128)(2,1)S(1)} %bitcast.10, f32[1,32]{1,0:T(1,128)S(1)} %bitcast.14, ...), custom_call_target="tpu_custom_call" | custom-call | tf_op jit(solution)/shard_map/pallas_call | solution.py:611
  (1 shorter events, 0.0 us)
Async XLA Ops:
  0.6 86.3 %slice-start = ((s8[6553600]{0:T(1024)(128)(4,1)}), s8[4194304]{0:T(1024)(128)(4,1)S(1)}, s32[]{:S(2)}) async-start(s8[6553600]{0:T(1024)(128)(4,1)} %bitcast.9), calls=%async_computation | async-start | bytes 8388608
  0.6 86.3 %slice-start.1 = ((s8[6553600]{0:T(1024)(128)(4,1)}), s8[2359296]{0:T(1024)(128)(4,1)S(1)}, s32[]{:S(2)}) async-start(s8[6553600]{0:T(1024)(128)(4,1)} %bitcast.9), calls=%async_computation.1 | async-start | bytes 4718592
  0.7 86.3 %copy-start = (bf16[1,20,64,640]{3,2,1,0:T(8,128)(2,1)S(1)}, bf16[1,20,64,640]{3,2,1,0:T(8,128)(2,1)}, u32[]{:S(2)}) copy-start(bf16[1,20,64,640]{3,2,1,0:T(8,128)(2,1)} %param.10) | copy-start | bytes 4915204
  0.7 86.3 %copy-start.3 = (f32[32]{0:T(128)S(1)}, f32[32]{0:T(128)}, u32[]{:S(2)}) copy-start(f32[32]{0:T(128)} %param.13) | copy-start | bytes 388
  86.9 1.1 %copy-start.1 = (bf16[20,64,256]{2,1,0:T(8,128)(2,1)S(1)}, bf16[20,64,256]{2,1,0:T(8,128)(2,1)}, u32[]{:S(2)}) copy-start(bf16[20,64,256]{2,1,0:T(8,128)(2,1)} %get-tuple-element.10.a_ref) | copy-start | bytes 1966084
  88.0 0.9 copy-start.2

commit v4 on v3

--- a/solution.py
+++ b/solution.py
@@ -30,7 +30,7 @@
 ARRIVE = ((0, 1, 2), (3,), (4,), (5,))
 BACK = ((0, 32), (32, 48), (48, 80))
 GR = 17
-STEP = 4
+STEP = 10
 VMEM_LIMIT = 54 * 2**20
 
 
@@ -157,7 +157,6 @@
             copy.start()
 
     tab_copy = pltpu.make_async_copy(tab_hbm, tab, tab_sem)
-    tab_copy.start()
 
     for copy in small:
         copy.wait()
@@ -219,14 +218,19 @@
             device_id_type=MESH,
         ).start()
 
-    def far_then_near(f):
+    def far(f):
         @pl.loop(0, LAT // 2)
         def _(i):
             f(peer(2 * i + 1))
 
+    def near(f):
         @pl.loop(1, LAT // 2)
         def _(i):
             f(peer(2 * i))
+
+    def far_then_near(f):
+        far(f)
+        near(f)
 
     def forward(n, ready=False):
         def f(d):
@@ -248,12 +252,13 @@
     pl.loop(8, 16)(legendre)
     forward(1)
     pl.loop(16, MB)(legendre)
+    tab_copy.start()
     forward(2)
     forward(3)
+    forward(4)
 
     @pl.loop(0, LAT)
     def _(d):
-        assemble(4, d)
         assemble(5, d)
 
     wp[...] = jnp.zeros_like(wp)
@@ -368,12 +373,14 @@
             stage[pl.ds(MB * q, MB), :] = rall[pl.ds(640 * q + d, MB, stride=LAT), :]
         bsnd[d, pl.ds(lo, hi - lo), :] = stage[pl.ds(lo, hi - lo), :].astype(BF16)
 
-    def back(n, ready=False):
+    def back(n):
         lo, hi = BACK[n]
 
         def go(d):
-            if not ready:
-                pack(n, d)
+            pack(n, d)
+            go_packed(d)
+
+        def go_packed(d):
             pltpu.make_async_remote_copy(
                 src_ref=bsnd.at[d, pl.ds(lo, hi - lo)],
                 dst_ref=brcv.at[me, pl.ds(lo, hi - lo)],
@@ -383,12 +390,18 @@
                 device_id_type=MESH,
             ).start()
 
-        far_then_near(go)
-        if not ready:
-            pack(n, me)
+        if n < 2:
+            far_then_near(go)
+        else:
+            near(go)
+        pack(n, me)
         pltpu.make_async_copy(
             bsnd.at[me, pl.ds(lo, hi - lo)], brcv.at[me, pl.ds(lo, hi - lo)], b_r.at[n]
         ).start()
+        if n == 2:
+            pl.loop(0, LAT // 2)(lambda i: pack(n, peer(2 * i + 1)))
+            reduce_2()
+            far(go_packed)
 
     def xy_step(n, src, dst, mine):
         @pl.loop(1, XY)
@@ -460,8 +473,8 @@
             @pl.when(c == now)
             def _():
                 arrive(now)
-                if now < 2:
-                    forward(now + 4, ready=True)
+                if now == 0:
+                    forward(5, ready=True)
 
         racc[...] = jnp.zeros_like(racc)
 
@@ -483,12 +496,7 @@
                 if now in (1, 2):
                     back(now - 1)
 
-    @pl.loop(0, LAT)
-    def _(d):
-        pack(2, d)
-
-    reduce_2()
-    back(2, ready=True)
+    back(2)
 
     def unpack(n):
         lo, hi = BACK[n]

time: 93.3 us -> 93.3 us (level)
  no operation moved by 1% of the time
where the time goes in v4:
time: 93.3 us; the launch traced here: 93.2 us
  Pallas kernels  90.5 us (97%)
  local copies, waits for them, and re-layouts  2.02 us (2%)
    pallas_call x1, Pallas kernels, body(): pl.pallas_call(kernel, out_shape=[jax.ShapeDtypeStruct((MB, 2 * CH, NP),...  86.9 us
    pallas_call x1, Pallas kernels, body(): pl.pallas_call(inverse_kernel, grid=(MB // STEP,), out_shape=[jax.ShapeDt...  3.52 us
    unnamed x12, local copies, waits for them, and re-layouts  2.02 us

profile of v4, /device:TPU:1, one launch (start us, length us, event | category | flops | bytes accessed | tf_op | source)
XLA Modules:
  0.0 93.2 jit_solution(3971906150870801788)
XLA Ops:
  0.6 0.0 slice-start
  0.6 0.0 slice-start.1
  0.7 0.0 copy-start
  0.7 0.0 copy-start.3
  0.7 86.9 %shard_map.120 = (bf16[20,64,256]{2,1,0:T(8,128)(2,1)}, f32[16,17,128]{2,1,0:T(8,128)}) custom-call(bf16[20,64,640]{2,1,0:T(8,128)(2,1)} %bitcast.15, bf16[20,64,640]{2,1,0:T(8,128)(2,1)} %bitcast.11, bf16[20,640,256]{2,1,0:T(8,128)(2,1)} %leg_ref.1, bf16[2,1280,640]{2,1,0:T(8,128)(2,1)} %constant.2.clone.tab_hbm, f32[1,256]{1,0:T(1,128)} %bitcast.18, ...), custom_call_target="tpu_custom_call" | custom-call | tf_op jit(solution)/shard_map/pallas_call | solution.py:594
  87.6 0.0 slice-done
  87.6 0.0 slice-done.1
  87.6 0.0 copy-done
  87.6 0.0 copy-done.3
  87.7 0.0 copy-start.1
  87.7 1.1 %copy-done.1 = bf16[20,64,256]{2,1,0:T(8,128)(2,1)S(1)} copy-done((bf16[20,64,256]{2,1,0:T(8,128)(2,1)S(1)}, bf16[20,64,256]{2,1,0:T(8,128)(2,1)}, u32[]{:S(2)}) %copy-start.1) | copy-done | bytes 655384
  88.7 0.0 copy-start.2
  88.7 0.9 copy-done.2
  89.7 3.5 %shard_map.121 = (f32[20,64,640]{2,1,0:T(8,128)}, f32[32,512]{1,0:T(8,128)}, f32[1,512]{1,0:T(1,128)}, f32[32,512]{1,0:T(8,128)}) custom-call(bf16[20,64,256]{2,1,0:T(8,128)(2,1)S(1)} %copy-done.1, bf16[20,64,640]{2,1,0:T(8,128)(2,1)S(1)} %bitcast.12, bf16[20,640,256]{2,1,0:T(8,128)(2,1)S(1)} %bitcast.10, f32[1,32]{1,0:T(1,128)S(1)} %bitcast.14, ...), custom_call_target="tpu_custom_call" | custom-call | tf_op jit(solution)/shard_map/pallas_call | solution.py:619
  (1 shorter events, 0.0 us)
Async XLA Ops:
  0.6 87.0 %slice-start = ((s8[6553600]{0:T(1024)(128)(4,1)}), s8[4194304]{0:T(1024)(128)(4,1)S(1)}, s32[]{:S(2)}) async-start(s8[6553600]{0:T(1024)(128)(4,1)} %bitcast.9), calls=%async_computation | async-start | bytes 8388608
  0.6 87.0 %slice-start.1 = ((s8[6553600]{0:T(1024)(128)(4,1)}), s8[2359296]{0:T(1024)(128)(4,1)S(1)}, s32[]{:S(2)}) async-start(s8[6553600]{0:T(1024)(128)(4,1)} %bitcast.9), calls=%async_computation.1 | async-start | bytes 4718592
  0.7 87.0 %copy-start = (bf16[1,20,64,640]{3,2,1,0:T(8,128)(2,1)S(1)}, bf16[1,20,64,640]{3,2,1,0:T(8,128)(2,1)}, u32[]{:S(2)}) copy-start(bf16[1,20,64,640]{3,2,1,0:T(8,128)(2,1)} %param.10) | copy-start | bytes 4915204
  0.7 87.0 %copy-start.3 = (f32[32]{0:T(128)S(1)}, f32[32]{0:T(128)}, u32[]{:S(2)}) copy-start(f32[32]{0:T(128)} %param.13) | copy-start | bytes 388
  87.7 1.1 %copy-start.1 = (bf16[20,64,256]{2,1,0:T(8,128)(2,1)S(1)}, bf16[20,64,256]{2,1,0:T(8,128)(2,1)}, u32[]{:S(2)}) copy-start(bf16[20,64,256]{2,1,0:T(8,128)(2,1)} %get-tuple-element.10.a_ref) | copy-start | bytes 1966084
  88.7 0.9 copy-start.2

commit v5 on v4

--- a/solution.py
+++ b/solution.py
@@ -561,8 +561,8 @@
         pltpu.VMEM((MB, NL, NP), BF16),
         pltpu.VMEM((2, HALF, COLS), BF16),
         pltpu.VMEM((CH, NL), F32),
-        pltpu.VMEM((MB * NP, 128), F32),
-        pltpu.VMEM((80, 128), F32),
+        pltpu.VMEM((24 * NP, 128), F32),
+        pltpu.VMEM((96, 128), F32),
         pltpu.VMEM((LAT, 160, 128), BF16),
         pltpu.VMEM((LAT, 160, 128), BF16),
         pltpu.VMEM((LAT * 80, 128), F32),
@@ -570,7 +570,7 @@
         pltpu.VMEM((2, 256, 2 * HID), BF16),
         pltpu.VMEM((HALF // JT, 2, 2 * JT, HID), BF16),
         pltpu.VMEM((2, 64, COLS), F32),
-        pltpu.VMEM((4 * 640, 128), F32),
+        pltpu.VMEM((4 * 640 + 256, 128), F32),
         pltpu.VMEM((LAT, 80, 128), BF16),
         pltpu.VMEM((LAT, 80, 128), BF16),
         pltpu.VMEM((48, HID), F32),

time: 93.3 us -> 93.2 us (level)
  no operation moved by 1% of the time
where the time goes in v5:
time: 93.2 us; the launch traced here: 93.1 us
  Pallas kernels  90.3 us (97%)
  local copies, waits for them, and re-layouts  2.02 us (2%)
    pallas_call x1, Pallas kernels, body(): pl.pallas_call(kernel, out_shape=[jax.ShapeDtypeStruct((MB, 2 * CH, NP),...  86.8 us
    pallas_call x1, Pallas kernels, body(): pl.pallas_call(inverse_kernel, grid=(MB // STEP,), out_shape=[jax.ShapeDt...  3.51 us
    unnamed x12, local copies, waits for them, and re-layouts  2.02 us

profile of v5, /device:TPU:1, one launch (start us, length us, event | category | flops | bytes accessed | tf_op | source)
XLA Modules:
  0.0 93.1 jit_solution(14978759530470855834)
XLA Ops:
  0.6 0.0 slice-start
  0.6 0.0 slice-start.1
  0.7 0.0 copy-start
  0.7 0.0 copy-start.3
  0.7 86.8 %shard_map.120 = (bf16[20,64,256]{2,1,0:T(8,128)(2,1)}, f32[16,17,128]{2,1,0:T(8,128)}) custom-call(bf16[20,64,640]{2,1,0:T(8,128)(2,1)} %bitcast.15, bf16[20,64,640]{2,1,0:T(8,128)(2,1)} %bitcast.11, bf16[20,640,256]{2,1,0:T(8,128)(2,1)} %leg_ref.1, bf16[2,1280,640]{2,1,0:T(8,128)(2,1)} %constant.2.clone.tab_hbm, f32[1,256]{1,0:T(1,128)} %bitcast.18, ...), custom_call_target="tpu_custom_call" | custom-call | tf_op jit(solution)/shard_map/pallas_call | solution.py:594
  87.5 0.0 slice-done
  87.5 0.0 slice-done.1
  87.5 0.0 copy-done
  87.5 0.0 copy-done.3
  87.5 0.0 copy-start.1
  87.6 1.1 %copy-done.1 = bf16[20,64,256]{2,1,0:T(8,128)(2,1)S(1)} copy-done((bf16[20,64,256]{2,1,0:T(8,128)(2,1)S(1)}, bf16[20,64,256]{2,1,0:T(8,128)(2,1)}, u32[]{:S(2)}) %copy-start.1) | copy-done | bytes 655384
  88.6 0.0 copy-start.2
  88.6 0.9 copy-done.2
  89.6 3.5 %shard_map.121 = (f32[20,64,640]{2,1,0:T(8,128)}, f32[32,512]{1,0:T(8,128)}, f32[1,512]{1,0:T(1,128)}, f32[32,512]{1,0:T(8,128)}) custom-call(bf16[20,64,256]{2,1,0:T(8,128)(2,1)S(1)} %copy-done.1, bf16[20,64,640]{2,1,0:T(8,128)(2,1)S(1)} %bitcast.12, bf16[20,640,256]{2,1,0:T(8,128)(2,1)S(1)} %bitcast.10, f32[1,32]{1,0:T(1,128)S(1)} %bitcast.14, ...), custom_call_target="tpu_custom_call" | custom-call | tf_op jit(solution)/shard_map/pallas_call | solution.py:619
  (1 shorter events, 0.0 us)
Async XLA Ops:
  0.6 86.9 %slice-start = ((s8[6553600]{0:T(1024)(128)(4,1)}), s8[4194304]{0:T(1024)(128)(4,1)S(1)}, s32[]{:S(2)}) async-start(s8[6553600]{0:T(1024)(128)(4,1)} %bitcast.9), calls=%async_computation | async-start | bytes 8388608
  0.6 86.9 %slice-start.1 = ((s8[6553600]{0:T(1024)(128)(4,1)}), s8[2359296]{0:T(1024)(128)(4,1)S(1)}, s32[]{:S(2)}) async-start(s8[6553600]{0:T(1024)(128)(4,1)} %bitcast.9), calls=%async_computation.1 | async-start | bytes 4718592
  0.7 86.9 %copy-start = (bf16[1,20,64,640]{3,2,1,0:T(8,128)(2,1)S(1)}, bf16[1,20,64,640]{3,2,1,0:T(8,128)(2,1)}, u32[]{:S(2)}) copy-start(bf16[1,20,64,640]{3,2,1,0:T(8,128)(2,1)} %param.10) | copy-start | bytes 4915204
  0.7 86.9 %copy-start.3 = (f32[32]{0:T(128)S(1)}, f32[32]{0:T(128)}, u32[]{:S(2)}) copy-start(f32[32]{0:T(128)} %param.13) | copy-start | bytes 388
  87.5 1.1 %copy-start.1 = (bf16[20,64,256]{2,1,0:T(8,128)(2,1)S(1)}, bf16[20,64,256]{2,1,0:T(8,128)(2,1)}, u32[]{:S(2)}) copy-start(bf16[20,64,256]{2,1,0:T(8,128)(2,1)} %get-tuple-element.10.a_ref) | copy-start | bytes 1966084
  88.6 0.9 copy-start.2
